TPU v7x, 32 devices: a whole 2x2x4 slice. The times are simulated.
32 devices in a mesh: lon: 8 (over y, x, core), lat: 4 (over z).
Axes of the slice: x: 2, y: 2, z: 4, core: 2. Of those that a mesh axis runs over, the one named last changes fastest.
Arguments:
- tokens: bfloat16 [1, 2, 168, 96, 512], P(None, None, 'lat', 'lon'), may hold values from -200 to 200
- group_ids: int32 [168, 96], replicated, may hold values from 0 to 1
- bias_table: float32 [759, 16], replicated, may hold values from -4 to 4
- w_qkv: bfloat16 [512, 1536], replicated, may hold values from -0.25 to 0.25
- w_proj: bfloat16 [512, 512], replicated, may hold values from -0.25 to 0.25
- gain_attn: float32 [512], replicated, may hold values from 0.5 to 1.5
- w_in: bfloat16 [512, 2048], replicated, may hold values from -0.25 to 0.25
- w_out: bfloat16 [2048, 512], replicated, may hold values from -0.125 to 0.125
- gain_mlp: float32 [512], replicated, may hold values from 0.5 to 1.5
Outputs:
- result: bfloat16 [1, 2, 168, 96, 512], P(None, None, 'lat', 'lon')
All inputs are finite; a program needn't handle non-finite values.
Results may differ from a plain program's by a relative error of at most 0.0085.
Values may be sent and summed in bfloat16 or wider, within the bound.
No kernel may reach another device: no remote copies, remote signals or barrier semaphores. Data moves between devices by JAX's collectives and lax.ppermute only.
A program may use at most 128 MiB of HBM per device.

v0:
```python
import functools

import jax
import jax.numpy as jnp
from jax import lax
from jax.experimental import pallas as pl
from jax.experimental.pallas import tpu as pltpu
from jax.sharding import PartitionSpec as P

WIN_LEV = 2
WIN_LAT = 6
WIN_LON = 12
SHIFT_LAT = 3
SHIFT_LON = 6

EPS = 1e-05
LOG2E = 1.4426950408889634
HALF = WIN_LEV * WIN_LAT * SHIFT_LON
ROW = WIN_LEV * SHIFT_LON
EDGE = SHIFT_LAT * ROW
KEYS = 2 * HALF
LANES = 256
GROUP = 4
VMEM_LIMIT = 50 * 1024 * 1024

F32 = jnp.float32
BF16 = jnp.bfloat16


def params():
    return pltpu.CompilerParams(vmem_limit_bytes=VMEM_LIMIT)


def vmem(count):
    return [pl.BlockSpec(memory_space=pltpu.VMEM)] * count


def pack_kernel(par_ref, tok_ref, near_ref, far_ref, top_ref, bot_ref, scr):
    lev, lat = tok_ref.shape[0], tok_ref.shape[1]
    par = par_ref[0]
    for h in range(lat):
        for z in range(lev):
            x = tok_ref[z, h].astype(F32)
            off = h * ROW + z * SHIFT_LON
            scr[1 - par, off : off + SHIFT_LON, :] = x[:SHIFT_LON]
            scr[par, off : off + SHIFT_LON, :] = x[SHIFT_LON:]
    rows = lat * ROW
    near_ref[...] = scr[0, EDGE : rows - EDGE, :].astype(BF16)
    far_ref[...] = scr[1, EDGE : rows - EDGE, :].astype(BF16)
    for side in range(2):
        top_ref[side] = scr[side, :EDGE, :].astype(BF16)
        bot_ref[side] = scr[side, rows - EDGE :, :].astype(BF16)


def pack(par, tokens):
    lev, lat, lon, d = tokens.shape
    main = (lat - 2 * SHIFT_LAT) * ROW
    return pl.pallas_call(
        pack_kernel,
        in_specs=[pl.BlockSpec(memory_space=pltpu.SMEM)] + vmem(1),
        out_specs=vmem(4),
        out_shape=[
            jax.ShapeDtypeStruct((main, d), BF16),
            jax.ShapeDtypeStruct((main, d), BF16),
            jax.ShapeDtypeStruct((2, EDGE, d), BF16),
            jax.ShapeDtypeStruct((2, EDGE, d), BF16),
        ],
        scratch_shapes=[pltpu.VMEM((2, lat * ROW, d), F32)],
        compiler_params=params(),
        name="pack",
    )(par, tokens)


def unpack_kernel(par_ref, near_ref, far_ref, edge_ref, out_ref, scr):
    lev, lat = out_ref.shape[0], out_ref.shape[1]
    par = par_ref[0]
    rows = lat * ROW
    mid = near_ref.shape[0]
    scr[0, EDGE : EDGE + mid, :] = near_ref[...].astype(F32)
    scr[1, EDGE : EDGE + mid, :] = far_ref[...].astype(F32)
    for side in range(2):
        part = edge_ref[side].astype(F32)
        scr[side, :EDGE, :] = part[4 : 4 + EDGE]
        scr[side, rows - EDGE :, :] = part[4 + EDGE : 4 + 2 * EDGE]
    for h in range(lat):
        for z in range(lev):
            off = h * ROW + z * SHIFT_LON
            left = scr[1 - par, off : off + SHIFT_LON, :]
            right = scr[par, off : off + SHIFT_LON, :]
            out_ref[z, h] = jnp.concatenate([left, right], 0).astype(BF16)


def unpack(par, near, far, edge, shape):
    lev, lat, lon, d = shape
    return pl.pallas_call(
        unpack_kernel,
        in_specs=[pl.BlockSpec(memory_space=pltpu.SMEM)] + vmem(3),
        out_specs=vmem(1)[0],
        out_shape=jax.ShapeDtypeStruct(shape, BF16),
        scratch_shapes=[pltpu.VMEM((2, lat * ROW, d), F32)],
        compiler_params=params(),
        name="unpack",
    )(par, near, far, edge)


def bias_kernel(e_ref, out_ref):
    heads = out_ref.shape[1]
    out_ref[...] = jnp.zeros_like(out_ref)
    for h in range(WIN_LAT):
        start = (WIN_LAT - 1 - h) * ROW
        own = e_ref[0, :, :, start : start + HALF]
        for side in range(2):
            halo = e_ref[1 + side, :, :, start : start + HALF]
            out_ref[side, :, h * ROW : (h + 1) * ROW, :HALF] = own
            out_ref[side, :, h * ROW : (h + 1) * ROW, HALF:KEYS] = halo


def expand_bias(even, bias_table):
    heads = bias_table.shape[1]
    nz, nh, nw = 2 * WIN_LEV - 1, 2 * WIN_LAT - 1, 2 * WIN_LON - 1
    wide = 2 * SHIFT_LON - 1
    flip = (jnp.transpose(bias_table[::-1], (1, 0)) * LOG2E).reshape(heads, nz, nh, nw)
    flip = jnp.transpose(flip, (0, 2, 1, 3))
    mine = flip[..., SHIFT_LON : SHIFT_LON + wide]
    ahead = flip[..., 2 * SHIFT_LON : 2 * SHIFT_LON + wide]
    behind = flip[..., :wide]
    kinds = jnp.stack(
        [mine, jnp.where(even, ahead, behind), jnp.where(even, behind, ahead)]
    )
    parts = []
    for z in range(WIN_LEV):
        for w in range(SHIFT_LON):
            parts.append(
                kinds[
                    :,
                    :,
                    :,
                    WIN_LEV - 1 - z : 2 * WIN_LEV - 1 - z,
                    SHIFT_LON - 1 - w : 2 * SHIFT_LON - 1 - w,
                ].reshape(3, heads, nh * ROW)
            )
    spread = jnp.stack(parts, axis=2)
    return pl.pallas_call(
        bias_kernel,
        in_specs=vmem(1),
        out_specs=vmem(1)[0],
        out_shape=jax.ShapeDtypeStruct((2, heads, HALF, LANES), F32),
        compiler_params=params(),
        name="bias",
    )(spread)


def label_masks(even, group_ids, lat_start, lon_start, lat_rows, lon_cols):
    total_lat = group_ids.shape[0]
    rows = jnp.arange(total_lat, dtype=jnp.int32)
    label = group_ids * 2 + (rows >= total_lat - SHIFT_LAT).astype(jnp.int32)[:, None]
    label = jnp.concatenate([label[-2 * SHIFT_LAT :], label], 0)
    label = jnp.concatenate([label[:, -WIN_LON:], label], 1)
    part = lax.dynamic_slice(
        label, (lat_start, lon_start), (lat_rows + 2 * SHIFT_LAT, lon_cols + WIN_LON)
    )
    s = SHIFT_LON
    left = jnp.concatenate([part[:, s : 2 * s], part[:, :s]], 1)
    right = part[:, 2 * s :]
    sides = jnp.stack([jnp.where(even, right, left), jnp.where(even, left, right)])
    wins = sides.shape[1] // WIN_LAT
    sides = sides.reshape(2, wins, WIN_LAT, 2, 1, s)
    sides = jnp.broadcast_to(sides, (2, wins, WIN_LAT, 2, WIN_LEV, s))
    sides = jnp.transpose(sides, (0, 1, 3, 2, 4, 5)).reshape(2, wins, KEYS)
    keys = jnp.pad(sides, ((0, 0), (0, 0), (0, LANES - KEYS)), constant_values=-1)
    same = sides[:, :, :HALF, None] == keys[:, :, None, :]
    return jnp.where(same, 0.0, -jnp.inf).astype(F32)


def norm_rows(value, gain):
    mean = jnp.mean(value, -1, keepdims=True)
    centred = value - mean
    var = jnp.mean(centred * centred, -1, keepdims=True)
    return centred * lax.rsqrt(var + EPS) * gain


def gelu(x):
    return 0.5 * x * (1.0 + lax.erf(x * 0.7071067811865476))


def layer_kernel(
    sides, wins, q_lo, q_rows, *refs
):
    refs = list(refs)
    own = [refs.pop(0) for _ in range(sides)]
    halo = [refs.pop(0) for _ in range(sides)]
    mask_ref, bias_ref, w_qkv, w_proj, gain_attn, w_in, w_out, gain_mlp, out_ref = refs[:9]
    q_scr, k_scr, v_scr, o_scr, mid_scr, acc_scr = refs[9:]
    d = w_proj.shape[0]
    heads = bias_ref.shape[1]
    hd = d // heads
    lanes = GROUP * hd
    groups = heads // GROUP
    per = q_rows // wins
    scale = LOG2E / hd**0.5

    k_scr[:, KEYS:, :] = jnp.zeros((sides * wins, LANES - KEYS, d), BF16)
    v_scr[:, KEYS:, :] = jnp.zeros((sides * wins, LANES - KEYS, 2 * d), BF16)
    for g in range(groups):
        v_scr[:, :, (2 * g + 1) * lanes : (2 * g + 2) * lanes] = jnp.ones((sides * wins, LANES, lanes), BF16)
    step = 2 * lanes
    for s in range(sides):
        xq = own[s][...] if q_rows == own[s].shape[0] else own[s][q_lo : q_lo + q_rows, :]
        for c in range(0, d, step):
            q = jnp.dot(xq, w_qkv[:, c : c + step], preferred_element_type=F32)
            q_scr[s * q_rows : (s + 1) * q_rows, c : c + step] = q * scale
        for c in range(0, d, step):
            for base in (d, 2 * d):
                w = w_qkv[:, base + c : base + c + step]
                a = jnp.dot(own[s][...], w, preferred_element_type=F32)
                b = jnp.dot(halo[s][...], w, preferred_element_type=F32)
                for i in range(wins):
                    both = jnp.concatenate(
                        [a[i * HALF : (i + 1) * HALF], b[i * HALF : (i + 1) * HALF]], 0
                    ).astype(BF16)
                    if base == d:
                        k_scr[s * wins + i, :KEYS, c : c + step] = both
                    else:
                        v_scr[s * wins + i, :KEYS, 2 * c : 2 * c + lanes] = both[:, :lanes]
                        v_scr[s * wins + i, :KEYS, 2 * c + step : 2 * c + step + lanes] = both[:, lanes:]

    lane_head = lax.broadcasted_iota(jnp.int32, (per, lanes), 1) // hd

    def window(s, i):
        first = (q_lo + i * per) - i * HALF
        wi = s * wins + i
        qs = s * q_rows + i * per
        if not isinstance(i, int):
            qs = pl.multiple_of(qs, 8)
            first = 0
        mask = mask_ref[wi, first : first + per, :]
        mask = jnp.concatenate([mask] * GROUP, 0)
        for g in range(groups):
            q = q_scr[pl.ds(qs, per), g * lanes : (g + 1) * lanes]
            lhs = jnp.concatenate(
                [jnp.where(lane_head == j, q, 0.0) for j in range(GROUP)], 0
            ).astype(BF16)
            k = k_scr[wi, :, g * lanes : (g + 1) * lanes]
            sc = lax.dot_general(lhs, k, (((1,), (1,)), ((), ())), preferred_element_type=F32)
            bias = bias_ref[s, g * GROUP : (g + 1) * GROUP, first : first + per, :]
            sc = sc + bias.reshape(GROUP * per, LANES) + mask
            top = jnp.max(sc, -1, keepdims=True)
            p = jnp.exp2(sc - top).astype(BF16)
            o = jnp.dot(p, v_scr[wi, :, 2 * g * lanes : (2 * g + 2) * lanes], preferred_element_type=F32)
            num, den = o[:per, :lanes], o[:per, lanes:]
            for j in range(1, GROUP):
                here = lane_head == j
                num = jnp.where(here, o[j * per : (j + 1) * per, :lanes], num)
                den = jnp.where(here, o[j * per : (j + 1) * per, lanes:], den)
            o_scr[pl.ds(qs, per), g * lanes : (g + 1) * lanes] = num / den

    for s in range(sides):
        if per == HALF:
            lax.fori_loop(0, wins, lambda i, c, s=s: (window(s, i), c)[1], 0)
        else:
            for i in range(wins):
                window(s, i)

    total = sides * q_rows
    proj = jnp.dot(o_scr[...].astype(BF16), w_proj[...], preferred_element_type=F32)
    branch = norm_rows(proj, gain_attn[...]).astype(BF16).astype(F32)
    for s in range(sides):
        x = own[s][...] if q_rows == own[s].shape[0] else own[s][q_lo : q_lo + q_rows, :]
        mid_scr[s * q_rows : (s + 1) * q_rows, :] = (
            x.astype(F32) + branch[s * q_rows : (s + 1) * q_rows]
        ).astype(BF16)
    ff = w_in.shape[1]
    chunk = 256
    for c in range(0, ff, chunk):
        up = jnp.dot(mid_scr[...], w_in[:, c : c + chunk], preferred_element_type=F32)
        hid = gelu(up).astype(BF16)
        down = jnp.dot(hid, w_out[c : c + chunk, :], preferred_element_type=F32)
        if c == 0:
            acc_scr[...] = down
        else:
            acc_scr[...] += down
    res = mid_scr[...].astype(F32) + norm_rows(acc_scr[...], gain_mlp[...])
    for s in range(sides):
        part = res[s * q_rows : (s + 1) * q_rows].astype(BF16)
        if sides == 1:
            out_ref[...] = part
        else:
            out_ref[s] = part


def layer(name, own, halo, mask, bias, weights, q_lo, q_rows):
    sides = len(own)
    wins = own[0].shape[0] // HALF
    d = own[0].shape[1]
    shape = (q_rows, d) if sides == 1 else (sides, q_rows, d)
    total = sides * q_rows
    return pl.pallas_call(
        functools.partial(layer_kernel, sides, wins, q_lo, q_rows),
        in_specs=vmem(2 * sides + 2 + len(weights)),
        out_specs=vmem(1)[0],
        out_shape=jax.ShapeDtypeStruct(shape, BF16),
        scratch_shapes=[
            pltpu.VMEM((total, d), F32),
            pltpu.VMEM((sides * wins, LANES, d), BF16),
            pltpu.VMEM((sides * wins, LANES, 2 * d), BF16),
            pltpu.VMEM((total, d), F32),
            pltpu.VMEM((total, d), BF16),
            pltpu.VMEM((total, d), F32),
        ],
        compiler_params=params(),
        name=name,
    )(*own, *halo, mask, bias, *weights)


def per_device(tokens, group_ids, bias_table, w_qkv, w_proj, gain_attn, w_in, w_out, gain_mlp):
    lat_rows = tokens.shape[2]
    lon_cols = tokens.shape[3]
    lon_count = lax.axis_size("lon")
    lat_count = lax.axis_size("lat")
    lon_at = lax.axis_index("lon")
    par = lax.rem(lon_at, 2).astype(jnp.int32)
    even = par == 0
    near_pairs = [(i, i ^ 1) for i in range(lon_count)]
    far_pairs = [(i, (i + (1 if i % 2 else -1)) % lon_count) for i in range(lon_count)]
    down_pairs = [(i, (i + 1) % lat_count) for i in range(lat_count)]
    up_pairs = [(i, (i - 1) % lat_count) for i in range(lat_count)]

    near, far, top, bot = pack(par.reshape(1), tokens[0])
    far_halo = lax.ppermute(far, "lon", far_pairs)
    near_halo = lax.ppermute(near, "lon", near_pairs)
    above = lax.ppermute(bot, "lat", down_pairs)
    below = lax.ppermute(top, "lat", up_pairs)
    edge = [jnp.concatenate([above[s], top[s], bot[s], below[s]], 0) for s in range(2)]
    edge_halo = [
        lax.ppermute(edge[0], "lon", near_pairs),
        lax.ppermute(edge[1], "lon", far_pairs),
    ]
    bias = expand_bias(even, bias_table)
    mask = label_masks(
        even, group_ids, lax.axis_index("lat") * lat_rows, lon_at * lon_cols, lat_rows, lon_cols
    )
    wins = mask.shape[1]
    weights = [w_qkv, w_proj, gain_attn.reshape(1, -1), w_in, w_out, gain_mlp.reshape(1, -1)]
    rows = near.shape[0]
    res_near = layer("near", [near], [near_halo], mask[0, 1 : wins - 1], bias[:1], weights, 0, rows)
    res_far = layer("far", [far], [far_halo], mask[1, 1 : wins - 1], bias[1:], weights, 0, rows)
    edge_mask = jnp.stack([mask[:, 0], mask[:, wins - 1]], 1).reshape(4, HALF, LANES)
    res_edge = layer("edge", edge, edge_halo, edge_mask, bias, weights, 32, 80)
    out = unpack(par.reshape(1), res_near, res_far, res_edge, tokens.shape[1:])
    return out[None]


def solution(mesh):
    in_specs = (P(None, None, "lat", "lon", None), P(), P(), P(), P(), P(), P(), P(), P())
    out_specs = P(None, None, "lat", "lon", None)
    return jax.shard_map(
        per_device, mesh=mesh, in_specs=in_specs, out_specs=out_specs, check_vma=False
    )
```

profile of v0, /device:TPU:0, one launch (start us, length us, event | category | flops | bytes accessed | tf_op | source)
XLA Modules:
  0.0 98.8 jit_solution(5109706315482590446)
XLA Ops:
  0.0 1.5 %copy.72 = bf16[1,2,42,12,512]{4,3,2,1,0:T(8,128)(2,1)S(1)} copy(bf16[1,2,42,12,512]{4,1,3,2,0:T(2,128)(2,1)} %param.9) | data formatting | bytes 2064384 | tf_op args[0]
  1.5 1.3 %pack.1 = (bf16[432,512]{1,0:T(8,128)(2,1)}, bf16[432,512]{1,0:T(8,128)(2,1)}, bf16[2,36,512]{2,1,0:T(8,128)(2,1)S(1)}, bf16[2,36,512]{2,1,0:T(8,128)(2,1)S(1)}) custom-call(s32[1]{0:T(128)} %bitcast.par_ref, bf16[2,42,12,512]{3,2,1,0:T(8,128)(2,1)S(1)} %bitcast.70), custom_call_target="tpu_custom_call" | custom-call | tf_op jit(solution)/shard_map/pack/pallas_call | solution.py:58
  2.8 3.0 %collective-permute-start.2 = (bf16[2,36,512]{2,1,0:T(8,128)(2,1)S(1)}, bf16[2,36,512]{2,1,0:T(8,128)(2,1)}, u32[]{:S(2)}, u32[]{:S(2)}) collective-permute-start(bf16[2,36,512]{2,1,0:T(8,128)(2,1)S(1)} %get-tuple-element.11), channel_id=1, source_target_pairs={{0,1},{1,2},{2,3},{3,0},{4,5},{5,6},{6,7},{7,4},{8,9},{9,10},{10,1... | collective-permute-start | bytes 221192 | tf_op jit(solution)/shard_map/ppermute | solution.py:331
  5.8 2.0 %collective-permute-start.3 = (bf16[2,36,512]{2,1,0:T(8,128)(2,1)S(1)}, bf16[2,36,512]{2,1,0:T(8,128)(2,1)}, u32[]{:S(2)}, u32[]{:S(2)}) collective-permute-start(bf16[2,36,512]{2,1,0:T(8,128)(2,1)S(1)} %get-tuple-element.12), channel_id=1, source_target_pairs={{0,3},{1,0},{2,1},{3,2},{4,7},{5,4},{6,5},{7,6},{8,11},{9,8},{10,9... | collective-permute-start | bytes 221192 | tf_op jit(solution)/shard_map/ppermute | solution.py:332
  7.9 1.6 %collective-permute-start.1 = (bf16[432,512]{1,0:T(8,128)(2,1)}, bf16[432,512]{1,0:T(8,128)(2,1)}, u32[]{:S(2)}, u32[]{:S(2)}) collective-permute-start(bf16[432,512]{1,0:T(8,128)(2,1)} %get-tuple-element.10.refs_0_), channel_id=1, source_target_pairs={{0,28},{4,8},{8,4},{12,16},{16,12},{20,24},{24,20},{28,0},{1,29},{... | collective-permute-start | bytes 1327112 | tf_op jit(solution)/shard_map/ppermute | solution.py:329
  9.7 0.4 reverse
  10.8 4.8 %fusion.4 = (f32[3,16,11,2,6]{4,2,3,1,0:T(8,128)S(1)}, f32[3,16,11,2,6]{4,2,3,1,0:T(8,128)S(1)}, f32[3,16,11,2,6]{4,2,3,1,0:T(8,128)S(1)}, f32[3,16,11,2,6]{4,2,...) fusion(f32[3,16,11,3,11]{4,2,3,1,0:T(8,128)S(1)} %pad_maximum_f, ...), kind=kLoop, calls=%fused_computation.35 | loop fusion | bytes 608256 | tf_op jit(solution)/shard_map/slice | solution.py:134
  15.7 2.3 %copy.46 = f32[3,16,11,2,6]{1,4,3,2,0:T(8,128)} copy(f32[3,16,11,2,6]{4,2,3,1,0:T(8,128)} %get-tuple-element.30) | data formatting | bytes 50688 | tf_op jit(solution)/shard_map/slice | solution.py:134
  18.0 1.0 stack_reshape.36
  18.9 0.8 copy.58
  19.7 2.3 %copy.47 = f32[3,16,11,2,6]{1,4,3,2,0:T(8,128)} copy(f32[3,16,11,2,6]{4,2,3,1,0:T(8,128)} %get-tuple-element.29) | data formatting | bytes 50688 | tf_op jit(solution)/shard_map/slice | solution.py:134
  22.0 1.0 stack_reshape.37
  23.0 0.7 copy.59
  23.7 2.3 %copy.48 = f32[3,16,11,2,6]{1,4,3,2,0:T(8,128)} copy(f32[3,16,11,2,6]{4,2,3,1,0:T(8,128)} %get-tuple-element.28) | data formatting | bytes 50688 | tf_op jit(solution)/shard_map/slice | solution.py:134
  26.0 1.0 stack_reshape.38
  27.0 0.8 copy.60
  27.8 2.3 %copy.49 = f32[3,16,11,2,6]{1,4,3,2,0:T(8,128)} copy(f32[3,16,11,2,6]{4,2,3,1,0:T(8,128)} %get-tuple-element.27) | data formatting | bytes 50688 | tf_op jit(solution)/shard_map/slice | solution.py:134
  30.1 1.0 stack_reshape.39
  31.1 0.8 copy.61
  31.8 2.3 %copy.50 = f32[3,16,11,2,6]{1,4,3,2,0:T(8,128)} copy(f32[3,16,11,2,6]{4,2,3,1,0:T(8,128)} %get-tuple-element.26) | data formatting | bytes 50688 | tf_op jit(solution)/shard_map/slice | solution.py:134
  34.1 1.0 stack_reshape.40
  35.1 0.8 copy.62
  35.9 2.3 %copy.51 = f32[3,16,11,2,6]{1,4,3,2,0:T(8,128)} copy(f32[3,16,11,2,6]{4,2,3,1,0:T(8,128)} %get-tuple-element.25) | data formatting | bytes 50688 | tf_op jit(solution)/shard_map/slice | solution.py:134
  38.2 1.0 stack_reshape.41
  39.2 0.8 copy.63
  40.0 2.3 %copy.52 = f32[3,16,11,2,6]{1,4,3,2,0:T(8,128)} copy(f32[3,16,11,2,6]{4,2,3,1,0:T(8,128)} %get-tuple-element.24) | data formatting | bytes 50688 | tf_op jit(solution)/shard_map/slice | solution.py:134
  42.3 1.0 stack_reshape.42
  43.3 0.7 copy.64
  44.0 2.3 %copy.53 = f32[3,16,11,2,6]{1,4,3,2,0:T(8,128)} copy(f32[3,16,11,2,6]{4,2,3,1,0:T(8,128)} %get-tuple-element.23) | data formatting | bytes 50688 | tf_op jit(solution)/shard_map/slice | solution.py:134
  46.3 1.0 stack_reshape.43
  47.3 0.8 copy.65
  48.0 1.2 %copy.54 = f32[3,16,11,2,6]{1,4,3,2,0:T(8,128)} copy(f32[3,16,11,2,6]{4,2,3,1,0:T(8,128)S(1)} %get-tuple-element.22) | data formatting | bytes 50688 | tf_op jit(solution)/shard_map/slice | solution.py:134
  49.2 1.0 stack_reshape.44
  50.4 0.5 copy.55
  51.0 0.5 copy.56
  51.8 0.5 copy.57
  52.6 1.5 %stack.34.e_ref = f32[3,16,12,132]{3,2,1,0:T(8,128)S(1)} concatenate(f32[3,16,1,132]{3,2,1,0:T(1,128)S(1)} %copy-done.5, f32[3,16,1,132]{3,2,1,0:T(1,128)S(1)} %copy-done.6, f32[3,16,1,132]{3,2,1,0:T(1,128)S(1)} %copy-done.7, f32[3,16,1,132]{3,2,1,0:T(1,128)S(1)} %copy-done.8, f32[3,16,1,132]{3,2,1,0:T(1,128)S(1)} %copy-done.9, f32[3,16,1,132]{3,2,1,0:T(1,128)S(1)} %copy-done.10, ...), dimensions={2} | concatenate | bytes 608256 | tf_op jit(solution)/shard_map/stack | solution.py:142
  54.1 0.8 bias.1.refs_5_
  56.8 0.9 slice_bitcast_fusion.4
  57.7 0.8 slice_bitcast_fusion.3
  58.6 0.4 collective-permute-start.4
  59.0 1.1 %collective-permute-start.5 = (bf16[144,512]{1,0:T(8,128)(2,1)S(1)}, bf16[144,512]{1,0:T(8,128)(2,1)S(1)}, u32[]{:S(2)}, u32[]{:S(2)}) collective-permute-start(bf16[144,512]{1,0:T(8,128)(2,1)S(1)} %pad_maximum_fusion.3.refs_1_), channel_id=1, source_target_pairs={{0,28},{4,8},{8,4},{12,16},{16,12},{20,24},{24,20},{28,0},{1,29},{... | collective-permute-start | bytes 442376 | tf_op jit(solution)/shard_map/ppermute | solution.py:336
  60.1 5.6 %collective-permute-done.5.refs_3_ = bf16[144,512]{1,0:T(8,128)(2,1)S(1)} collective-permute-done((bf16[144,512]{1,0:T(8,128)(2,1)S(1)}, bf16[144,512]{1,0:T(8,128)(2,1)S(1)}, u32[]{:S(2)}, u32[]{:S(2)}) %collective-permute-start.5) | collective-permute-done | bytes 147488 | tf_op jit(solution)/shard_map/ppermute | solution.py:336
  65.7 6.6 %edge.1.edge_ref = bf16[2,80,512]{2,1,0:T(8,128)(2,1)S(1)} custom-call(bf16[144,512]{1,0:T(8,128)(2,1)S(1)} %pad_maximum_fusion.2.refs_0_, bf16[144,512]{1,0:T(8,128)(2,1)S(1)} %pad_maximum_fusion.3.refs_1_, bf16[144,512]{1,0:T(8,128)(2,1)S(1)} %collective-permute-done.4.refs_2_, bf16[144,512]{1,0:T(8,128)(2,1)S(1)} %collective-permute-done.5.refs_3_, ...), custom_call_target="tpu_custom_call" | custom-call | tf_op jit(solution)/shard_map/edge/pallas_call | solution.py:297
  72.3 11.9 %far.1.far_ref = bf16[432,512]{1,0:T(8,128)(2,1)S(1)} custom-call(bf16[432,512]{1,0:T(8,128)(2,1)} %get-tuple-element.10.refs_0_, bf16[432,512]{1,0:T(8,128)(2,1)} %collective-permute-done.1.refs_1_, f32[6,72,256]{2,1,0:T(8,128)S(1)} %get-tuple-element.17.refs_2_, f32[1,16,72,256]{3,2,1,0:T(8,128)S(1)} %get-tuple-element.13.refs_3_, ...), custom_call_target="tpu_custom_call" | custom-call | tf_op jit(solution)/shard_map/far/pallas_call | solution.py:297
  84.2 12.0 %near.1.near_ref = bf16[432,512]{1,0:T(8,128)(2,1)S(1)} custom-call(bf16[432,512]{1,0:T(8,128)(2,1)} %get-tuple-element.9.refs_0_, bf16[432,512]{1,0:T(8,128)(2,1)} %collective-permute-done.refs_1_, f32[6,72,256]{2,1,0:T(8,128)S(1)} %get-tuple-element.18.refs_2_, f32[1,16,72,256]{3,2,1,0:T(8,128)S(1)} %get-tuple-element.14.refs_3_, ...), custom_call_target="tpu_custom_call" | custom-call | tf_op jit(solution)/shard_map/near/pallas_call | solution.py:297
  96.2 0.5 unpack.1
  96.8 2.0 %copy.70 = bf16[1,2,42,12,512]{4,1,3,2,0:T(2,128)(2,1)} copy(bf16[1,2,42,12,512]{4,3,2,1,0:T(8,128)(2,1)S(1)} %bitcast.71) | data formatting | bytes 2064384 | tf_op jit(solution)/shard_map/broadcast_in_dim | solution.py:350
  (71 shorter events, 3.4 us)
Async XLA Ops:
  1.5 8.2 %copy-start.14 = (f32[759,16]{0,1:T(8,128)S(1)}, f32[759,16]{0,1:T(8,128)}, u32[]{:S(2)}) copy-start(f32[759,16]{0,1:T(8,128)} %param.11) | copy-start | bytes 145732
  2.8 54.0 %collective-permute-start.2 = (bf16[2,36,512]{2,1,0:T(8,128)(2,1)S(1)}, bf16[2,36,512]{2,1,0:T(8,128)(2,1)}, u32[]{:S(2)}, u32[]{:S(2)}) collective-permute-start(bf16[2,36,512]{2,1,0:T(8,128)(2,1)S(1)} %get-tuple-element.11), channel_id=1, source_target_pairs={{0,1},{1,2},{2,3},{3,0},{4,5},{5,6},{6,7},{7,4},{8,9},{9,10},{10,1... | collective-permute-start | bytes 221192 | tf_op jit(solution)/shard_map/ppermute | solution.py:331
  5.8 51.9 %collective-permute-start.3 = (bf16[2,36,512]{2,1,0:T(8,128)(2,1)S(1)}, bf16[2,36,512]{2,1,0:T(8,128)(2,1)}, u32[]{:S(2)}, u32[]{:S(2)}) collective-permute-start(bf16[2,36,512]{2,1,0:T(8,128)(2,1)S(1)} %get-tuple-element.12), channel_id=1, source_target_pairs={{0,3},{1,0},{2,1},{3,2},{4,7},{5,4},{6,5},{7,6},{8,11},{9,8},{10,9... | collective-permute-start | bytes 221192 | tf_op jit(solution)/shard_map/ppermute | solution.py:332
  7.9 64.5 %collective-permute-start.1 = (bf16[432,512]{1,0:T(8,128)(2,1)}, bf16[432,512]{1,0:T(8,128)(2,1)}, u32[]{:S(2)}, u32[]{:S(2)}) collective-permute-start(bf16[432,512]{1,0:T(8,128)(2,1)} %get-tuple-element.10.refs_0_), channel_id=1, source_target_pairs={{0,28},{4,8},{8,4},{12,16},{16,12},{20,24},{24,20},{28,0},{1,29},{... | collective-permute-start | bytes 1327112 | tf_op jit(solution)/shard_map/ppermute | solution.py:329
  9.5 74.8 %collective-permute-start = (bf16[432,512]{1,0:T(8,128)(2,1)}, bf16[432,512]{1,0:T(8,128)(2,1)}, u32[]{:S(2)}, u32[]{:S(2)}) collective-permute-start(bf16[432,512]{1,0:T(8,128)(2,1)} %get-tuple-element.9.refs_0_), channel_id=1, source_target_pairs={{0,4},{4,0},{8,12},{12,8},{16,20},{20,16},{24,28},{28,24},{1,5},{5... | collective-permute-start | bytes 1327112 | tf_op jit(solution)/shard_map/ppermute | solution.py:330
  51.6 0.9 copy-start.5
  51.6 0.9 copy-start.6
  51.6 0.9 copy-start.7
  51.6 0.9 copy-start.8
  51.6 0.9 copy-start.9
  51.6 0.9 copy-start.10
  51.6 0.9 copy-start.11
  51.6 0.9 copy-start.12
  54.1 0.9 copy-start.13
  55.0 1.4 %copy-start = (f32[2,16,72,256]{3,2,1,0:T(8,128)}, f32[2,16,72,256]{3,2,1,0:T(8,128)S(1)}, u32[]{:S(2)}) copy-start(f32[2,16,72,256]{3,2,1,0:T(8,128)S(1)} %bias.1.refs_5_) | copy-start | bytes 7077892
  56.7 9.0 %copy-start.1 = (bf16[512,1536]{1,0:T(8,128)(2,1)S(1)}, bf16[512,1536]{1,0:T(8,128)(2,1)}, u32[]{:S(2)}) copy-start(bf16[512,1536]{1,0:T(8,128)(2,1)} %refs_6_.1) | copy-start | bytes 4718596
  56.7 9.0 %copy-start.2 = (bf16[512,512]{1,0:T(8,128)(2,1)S(1)}, bf16[512,512]{1,0:T(8,128)(2,1)}, u32[]{:S(2)}) copy-start(bf16[512,512]{1,0:T(8,128)(2,1)} %refs_7_.5) | copy-start | bytes 1572868
  56.7 9.0 %copy-start.3 = (f32[512]{0:T(512)S(1)}, f32[512]{0:T(512)}, u32[]{:S(2)}) copy-start(f32[512]{0:T(512)} %param.14) | copy-start | bytes 6148
  56.7 9.0 %copy-start.4 = (f32[512]{0:T(512)S(1)}, f32[512]{0:T(512)}, u32[]{:S(2)}) copy-start(f32[512]{0:T(512)} %param.17) | copy-start | bytes 6148
  58.6 1.6 %collective-permute-start.4 = (bf16[144,512]{1,0:T(8,128)(2,1)S(1)}, bf16[144,512]{1,0:T(8,128)(2,1)S(1)}, u32[]{:S(2)}, u32[]{:S(2)}) collective-permute-start(bf16[144,512]{1,0:T(8,128)(2,1)S(1)} %pad_maximum_fusion.2.refs_0_), channel_id=1, source_target_pairs={{0,4},{4,0},{8,12},{12,8},{16,20},{20,16},{24,28},{28,24},{1,5},{5... | collective-permute-start | bytes 442376 | tf_op jit(solution)/shard_map/ppermute | solution.py:335
  59.0 6.7 %collective-permute-start.5 = (bf16[144,512]{1,0:T(8,128)(2,1)S(1)}, bf16[144,512]{1,0:T(8,128)(2,1)S(1)}, u32[]{:S(2)}, u32[]{:S(2)}) collective-permute-start(bf16[144,512]{1,0:T(8,128)(2,1)S(1)} %pad_maximum_fusion.3.refs_1_), channel_id=1, source_target_pairs={{0,28},{4,8},{8,4},{12,16},{16,12},{20,24},{24,20},{28,0},{1,29},{... | collective-permute-start | bytes 442376 | tf_op jit(solution)/shard_map/ppermute | solution.py:336
where the time goes:
time: 99.7 us; the launch traced here: 98.8 us
  local copies, waits for them, and re-layouts  50.3 us (50%)
  Pallas kernels  33.1 us (33%)
  starting transfers between devices  8.34 us (8%)
  waiting for transfers between devices  5.57 us (6%)
    pallas_call x3, Pallas kernels, layer(): pl.pallas_call(functools.partial(layer_kernel, sides, wins, q_lo, q_rows)...  30.5 us
    slice x13, local copies, waits for them, and re-layouts, expand_bias(): kinds[:, :, :, WIN_LEV - 1 - z:2 * WIN_LEV - 1 - z, SHIFT_LON - 1 - w:2 *...  26.1 us
    another operation x25, local copies, waits for them, and re-layouts, expand_bias(): spread = jnp.stack(parts, axis=2)  17 us
    ppermute x1, waiting for transfers between devices, per_device(): lax.ppermute(edge[1], 'lon', far_pairs)  5.56 us
    ppermute x1, starting transfers between devices, per_device(): above = lax.ppermute(bot, 'lat', down_pairs)  3.02 us
    unnamed x33, local copies, waits for them, and re-layouts  2.12 us
    ppermute x1, starting transfers between devices, per_device(): below = lax.ppermute(top, 'lat', up_pairs)  2.03 us
    broadcast_in_dim x1, local copies, waits for them, and re-layouts, per_device(): return out[None]  2.02 us
  transfers between devices with their start and end apart: 6, of which 1 were waited for; matrix products, arithmetic and copies ran while one was open for 48% of the time, Pallas kernels for 20%

commit v1 on v0

v1 whole, which is shorter than its diff:
```python
import functools

import jax
import jax.numpy as jnp
import numpy as np
from jax import lax
from jax.experimental import pallas as pl
from jax.experimental.pallas import tpu as pltpu
from jax.sharding import PartitionSpec as P

WIN_LEV = 2
WIN_LAT = 6
WIN_LON = 12
SHIFT_LAT = 3
SHIFT_LON = 6

EPS = 1e-05
LOG2E = 1.4426950408889634
HALF = WIN_LEV * WIN_LAT * SHIFT_LON
ROW = WIN_LEV * SHIFT_LON
EDGE = SHIFT_LAT * ROW
KEYS = 2 * HALF
LANES = 256
GROUP = 4
PACK_CHUNKS = 6
VMEM_LIMIT = 50 * 1024 * 1024

F32 = jnp.float32
BF16 = jnp.bfloat16


def params():
    return pltpu.CompilerParams(vmem_limit_bytes=VMEM_LIMIT)


def vmem(count):
    return [pl.BlockSpec(memory_space=pltpu.VMEM)] * count


def pack_kernel(par_ref, tok_ref, near_ref, far_ref, top_ref, bot_ref, buf, main, ends, sems):
    cells = tok_ref.shape[0]
    lat = main.shape[1] // ROW + 2 * SHIFT_LAT
    wide = cells // lat
    par = par_ref[0]
    each = cells // PACK_CHUNKS
    copies = [
        pltpu.make_async_copy(
            tok_ref.at[pl.ds(i * each, each)], buf.at[pl.ds(i * each, each)], sems.at[i]
        )
        for i in range(PACK_CHUNKS)
    ]
    for copy in copies:
        copy.start()
    waited = 0
    for h in range(lat):
        while waited < PACK_CHUNKS and waited * each < (h + 1) * wide:
            copies[waited].wait()
            waited += 1
        for half in range(2):
            at = h * wide + half * SHIFT_LON
            x = buf[at : at + SHIFT_LON].astype(F32).reshape(ROW, buf.shape[2])
            side = par if half else 1 - par
            if h < SHIFT_LAT:
                ends[side, h * ROW : (h + 1) * ROW, :] = x
            elif h >= lat - SHIFT_LAT:
                off = 40 + (h - lat + SHIFT_LAT) * ROW
                ends[side, off : off + ROW, :] = x
            else:
                off = (h - SHIFT_LAT) * ROW
                main[side, off : off + ROW, :] = x
    near_ref[...] = main[0].astype(BF16)
    far_ref[...] = main[1].astype(BF16)
    for side in range(2):
        top_ref[side] = ends[side, :EDGE, :].astype(BF16)
        bot_ref[side] = ends[side, 40 : 40 + EDGE, :].astype(BF16)


def pack(par, cells, lat):
    count, lev, d = cells.shape
    main = (lat - 2 * SHIFT_LAT) * ROW
    return pl.pallas_call(
        pack_kernel,
        in_specs=[pl.BlockSpec(memory_space=pltpu.SMEM), pl.BlockSpec(memory_space=pl.ANY)],
        out_specs=vmem(4),
        out_shape=[
            jax.ShapeDtypeStruct((main, d), BF16),
            jax.ShapeDtypeStruct((main, d), BF16),
            jax.ShapeDtypeStruct((2, EDGE, d), BF16),
            jax.ShapeDtypeStruct((2, EDGE, d), BF16),
        ],
        scratch_shapes=[
            pltpu.VMEM((count, lev, d), BF16),
            pltpu.VMEM((2, main, d), F32),
            pltpu.VMEM((2, 80, d), F32),
            pltpu.SemaphoreType.DMA((PACK_CHUNKS,)),
        ],
        compiler_params=params(),
        name="pack",
    )(par, cells)


def edge_pack_kernel(above_ref, top_ref, bot_ref, below_ref, near_ref, far_ref, scr):
    for side, out in enumerate((near_ref, far_ref)):
        for i, ref in enumerate((above_ref, top_ref, bot_ref, below_ref)):
            scr[i * EDGE : (i + 1) * EDGE, :] = ref[side].astype(F32)
        out[...] = scr[...].astype(BF16)


def edge_pack(above, top, bot, below):
    d = top.shape[2]
    return pl.pallas_call(
        edge_pack_kernel,
        in_specs=vmem(4),
        out_specs=vmem(2),
        out_shape=[jax.ShapeDtypeStruct((4 * EDGE, d), BF16)] * 2,
        scratch_shapes=[pltpu.VMEM((4 * EDGE, d), F32)],
        compiler_params=params(),
        name="edge_pack",
    )(above, top, bot, below)


def unpack_kernel(par_ref, near_ref, far_ref, edge_ref, out_ref, scr):
    par = par_ref[0]
    mid = near_ref.shape[0]
    rows = mid + 2 * EDGE
    lat = rows // ROW
    wide = out_ref.shape[0] // lat
    scr[0, EDGE : EDGE + mid, :] = near_ref[...].astype(F32)
    scr[1, EDGE : EDGE + mid, :] = far_ref[...].astype(F32)
    for side in range(2):
        part = edge_ref[side].astype(F32)
        scr[side, :EDGE, :] = part[4 : 4 + EDGE]
        scr[side, rows - EDGE :, :] = part[4 + EDGE : 4 + 2 * EDGE]
    for h in range(lat):
        for half in range(2):
            at = h * wide + half * SHIFT_LON
            side = par if half else 1 - par
            x = scr[side, h * ROW : (h + 1) * ROW, :]
            out_ref[at : at + SHIFT_LON] = x.reshape(SHIFT_LON, WIN_LEV, x.shape[1]).astype(BF16)


def unpack(par, near, far, edge, cells):
    d = near.shape[1]
    return pl.pallas_call(
        unpack_kernel,
        in_specs=[pl.BlockSpec(memory_space=pltpu.SMEM)] + vmem(3),
        out_specs=vmem(1)[0],
        out_shape=jax.ShapeDtypeStruct((cells, WIN_LEV, d), BF16),
        scratch_shapes=[pltpu.VMEM((2, near.shape[0] + 2 * EDGE, d), F32)],
        compiler_params=params(),
        name="unpack",
    )(par, near, far, edge)


def spread_matrix(count):
    nw, nh = 2 * WIN_LON - 1, 2 * WIN_LAT - 1
    out = np.zeros((count, 3, LANES), np.float32)
    for kind, centre in enumerate((WIN_LON - 1, SHIFT_LON - 1, WIN_LON + SHIFT_LON - 1)):
        for j in range(nh):
            for w in range(SHIFT_LON):
                for z in range(WIN_LEV):
                    at = (WIN_LEV - 1 - z) * nh * nw + (nh - 1 - j) * nw + centre - w
                    out[at, kind, j * ROW + w * WIN_LEV + z] = 1
    return out.reshape(count, 3 * LANES)


def prep_kernel(
    at_ref, gid_ref, table_ref, spread_ref, bias_near, bias_far, mask_near, mask_far, mask_edge, wide, kinds
):
    heads, offsets = table_ref.shape
    nw, nh = 2 * WIN_LON - 1, 2 * WIN_LAT - 1
    par, lat_at, lon_at = at_ref[0], at_ref[1], at_ref[2]
    count = wide.shape[1]
    wide[...] = jnp.zeros_like(wide)
    wide[:, :offsets] = table_ref[...] * LOG2E
    x = jnp.broadcast_to(wide[...][:, None, :], (heads, 16, count)).reshape(heads * 16, count)
    place = lax.broadcasted_iota(jnp.int32, x.shape, 0) % 16
    for amount, bit in ((nh * nw, place % 2), (1, place // 2 % 2), (2, place // 4 % 2), (4, place // 8)):
        x = jnp.where(bit == 1, pltpu.roll(x, count - amount, 1), x)
    high = x.astype(BF16)
    low = (x - high.astype(F32)).astype(BF16)
    for kind in range(3):
        m = spread_ref[:, kind * LANES : (kind + 1) * LANES]
        y = jnp.dot(high, m, preferred_element_type=F32) + jnp.dot(low, m, preferred_element_type=F32)
        kinds[kind] = y.reshape(heads, 16, LANES)
    for side, out in enumerate((bias_near, bias_far)):
        halo = kinds[2 - par if side else 1 + par]
        out[:, :, KEYS:] = jnp.zeros((heads, HALF, LANES - KEYS), F32)
        for h in range(WIN_LAT):
            start = (WIN_LAT - 1 - h) * ROW
            out[:, h * ROW : (h + 1) * ROW, :HALF] = kinds[0, :, :ROW, start : start + HALF]
            out[:, h * ROW : (h + 1) * ROW, HALF:KEYS] = halo[:, :ROW, start : start + HALF]
    total, around = gid_ref.shape
    wins = mask_near.shape[0] + 2
    lat_rows = (wins - 1) * WIN_LAT
    lane = lax.broadcasted_iota(jnp.int32, (1, LANES), 1)
    is_halo = lane >= HALF
    rest = jnp.where(is_halo, lane - HALF, lane)
    h_of = rest // ROW
    w_of = rest % ROW // WIN_LEV
    ids = gid_ref[...].astype(BF16)
    row = lax.broadcasted_iota(jnp.int32, (total, LANES), 0)
    col = lax.broadcasted_iota(jnp.int32, (around, LANES), 0)
    for side in range(2):
        right = par == side
        offset = jnp.where(
            right, jnp.where(is_halo, SHIFT_LON, 0), jnp.where(is_halo, -WIN_LON, -SHIFT_LON)
        )
        want = lon_at * 2 * SHIFT_LON + offset + w_of
        want = jnp.where(want < 0, want + around, want)
        pick = jnp.where(col == want, 1.0, 0.0).astype(BF16)
        label = 2.0 * jnp.dot(ids, pick, preferred_element_type=F32)
        label = label + jnp.where(row >= total - SHIFT_LAT, 1.0, 0.0)
        lines = []
        for k in range(wins):
            want = lat_at * lat_rows + (k - 1) * WIN_LAT + h_of
            want = jnp.where(want < 0, want + total, want)
            line = jnp.sum(jnp.where(row == want, label, 0.0), 0, keepdims=True)
            lines.append(jnp.where(lane < KEYS, line, -1.0))
        lines = jnp.concatenate(lines, 0)
        cols = lines[:, :128].T
        for k in range(wins):
            same = cols[:HALF, k : k + 1] == lines[k : k + 1, :]
            mask = jnp.where(same, 0.0, -jnp.inf)
            if k == 0:
                mask_edge[2 * side] = mask
            elif k == wins - 1:
                mask_edge[2 * side + 1] = mask
            elif side == 0:
                mask_near[k - 1] = mask
            else:
                mask_far[k - 1] = mask


def prep(at, group_ids, table, wins):
    heads, offsets = table.shape
    count = -(-offsets // LANES) * LANES
    spread = jnp.asarray(spread_matrix(count), BF16)
    return pl.pallas_call(
        prep_kernel,
        in_specs=[pl.BlockSpec(memory_space=pltpu.SMEM)] + vmem(3),
        out_specs=vmem(5),
        out_shape=[jax.ShapeDtypeStruct((heads, HALF, LANES), F32)] * 2
        + [jax.ShapeDtypeStruct((wins - 2, HALF, LANES), F32)] * 2
        + [jax.ShapeDtypeStruct((4, HALF, LANES), F32)],
        scratch_shapes=[
            pltpu.VMEM((heads, count), F32),
            pltpu.VMEM((3, heads, 16, LANES), F32),
        ],
        compiler_params=params(),
        name="prep",
    )(at, group_ids, table, spread)


def norm_rows(value, gain):
    mean = jnp.mean(value, -1, keepdims=True)
    centred = value - mean
    var = jnp.mean(centred * centred, -1, keepdims=True)
    return centred * lax.rsqrt(var + EPS) * gain


def gelu(x):
    return 0.5 * x * (1.0 + lax.erf(x * 0.7071067811865476))


def layer_kernel(
    sides, wins, q_lo, q_rows, *refs
):
    refs = list(refs)
    own = [refs.pop(0) for _ in range(sides)]
    halo = [refs.pop(0) for _ in range(sides)]
    bias = [refs.pop(0) for _ in range(sides)]
    mask_ref, w_qkv, w_proj, gain_attn, w_in, w_out, gain_mlp, out_ref = refs[:8]
    q_scr, k_scr, v_scr, o_scr, mid_scr, acc_scr = refs[8:]
    d = w_proj.shape[0]
    heads = bias[0].shape[0]
    hd = d // heads
    lanes = GROUP * hd
    groups = heads // GROUP
    per = q_rows // wins
    scale = LOG2E / hd**0.5

    k_scr[:, KEYS:, :] = jnp.zeros((sides * wins, LANES - KEYS, d), BF16)
    v_scr[:, KEYS:, :] = jnp.zeros((sides * wins, LANES - KEYS, 2 * d), BF16)
    for g in range(groups):
        v_scr[:, :, (2 * g + 1) * lanes : (2 * g + 2) * lanes] = jnp.ones((sides * wins, LANES, lanes), BF16)
    step = 2 * lanes
    for s in range(sides):
        xq = own[s][...] if q_rows == own[s].shape[0] else own[s][q_lo : q_lo + q_rows, :]
        for c in range(0, d, step):
            q = jnp.dot(xq, w_qkv[:, c : c + step], preferred_element_type=F32)
            q_scr[s * q_rows : (s + 1) * q_rows, c : c + step] = q * scale
        for c in range(0, d, step):
            for base in (d, 2 * d):
                w = w_qkv[:, base + c : base + c + step]
                a = jnp.dot(own[s][...], w, preferred_element_type=F32)
                b = jnp.dot(halo[s][...], w, preferred_element_type=F32)
                for i in range(wins):
                    both = jnp.concatenate(
                        [a[i * HALF : (i + 1) * HALF], b[i * HALF : (i + 1) * HALF]], 0
                    ).astype(BF16)
                    if base == d:
                        k_scr[s * wins + i, :KEYS, c : c + step] = both
                    else:
                        v_scr[s * wins + i, :KEYS, 2 * c : 2 * c + lanes] = both[:, :lanes]
                        v_scr[s * wins + i, :KEYS, 2 * c + step : 2 * c + step + lanes] = both[:, lanes:]

    lane_head = lax.broadcasted_iota(jnp.int32, (per, lanes), 1) // hd

    def window(s, i):
        first = (q_lo + i * per) - i * HALF
        wi = s * wins + i
        qs = s * q_rows + i * per
        if not isinstance(i, int):
            qs = pl.multiple_of(qs, 8)
            first = 0
        mask = mask_ref[wi, first : first + per, :]
        mask = jnp.concatenate([mask] * GROUP, 0)
        for g in range(groups):
            q = q_scr[pl.ds(qs, per), g * lanes : (g + 1) * lanes]
            lhs = jnp.concatenate(
                [jnp.where(lane_head == j, q, 0.0) for j in range(GROUP)], 0
            ).astype(BF16)
            k = k_scr[wi, :, g * lanes : (g + 1) * lanes]
            sc = lax.dot_general(lhs, k, (((1,), (1,)), ((), ())), preferred_element_type=F32)
            extra = bias[s][g * GROUP : (g + 1) * GROUP, first : first + per, :]
            sc = sc + extra.reshape(GROUP * per, LANES) + mask
            top = jnp.max(sc, -1, keepdims=True)
            p = jnp.exp2(sc - top).astype(BF16)
            o = jnp.dot(p, v_scr[wi, :, 2 * g * lanes : (2 * g + 2) * lanes], preferred_element_type=F32)
            num, den = o[:per, :lanes], o[:per, lanes:]
            for j in range(1, GROUP):
                here = lane_head == j
                num = jnp.where(here, o[j * per : (j + 1) * per, :lanes], num)
                den = jnp.where(here, o[j * per : (j + 1) * per, lanes:], den)
            o_scr[pl.ds(qs, per), g * lanes : (g + 1) * lanes] = num / den

    for s in range(sides):
        if per == HALF:
            lax.fori_loop(0, wins, lambda i, c, s=s: (window(s, i), c)[1], 0)
        else:
            for i in range(wins):
                window(s, i)

    total = sides * q_rows
    proj = jnp.dot(o_scr[...].astype(BF16), w_proj[...], preferred_element_type=F32)
    branch = norm_rows(proj, gain_attn[...]).astype(BF16).astype(F32)
    for s in range(sides):
        x = own[s][...] if q_rows == own[s].shape[0] else own[s][q_lo : q_lo + q_rows, :]
        mid_scr[s * q_rows : (s + 1) * q_rows, :] = (
            x.astype(F32) + branch[s * q_rows : (s + 1) * q_rows]
        ).astype(BF16)
    ff = w_in.shape[1]
    chunk = 256
    for c in range(0, ff, chunk):
        up = jnp.dot(mid_scr[...], w_in[:, c : c + chunk], preferred_element_type=F32)
        hid = gelu(up).astype(BF16)
        down = jnp.dot(hid, w_out[c : c + chunk, :], preferred_element_type=F32)
        if c == 0:
            acc_scr[...] = down
        else:
            acc_scr[...] += down
    res = mid_scr[...].astype(F32) + norm_rows(acc_scr[...], gain_mlp[...])
    for s in range(sides):
        part = res[s * q_rows : (s + 1) * q_rows].astype(BF16)
        if sides == 1:
            out_ref[...] = part
        else:
            out_ref[s] = part


def layer(name, own, halo, bias, mask, weights, q_lo, q_rows):
    sides = len(own)
    wins = own[0].shape[0] // HALF
    d = own[0].shape[1]
    shape = (q_rows, d) if sides == 1 else (sides, q_rows, d)
    total = sides * q_rows
    return pl.pallas_call(
        functools.partial(layer_kernel, sides, wins, q_lo, q_rows),
        in_specs=vmem(3 * sides + 1 + len(weights)),
        out_specs=vmem(1)[0],
        out_shape=jax.ShapeDtypeStruct(shape, BF16),
        scratch_shapes=[
            pltpu.VMEM((total, d), F32),
            pltpu.VMEM((sides * wins, LANES, d), BF16),
            pltpu.VMEM((sides * wins, LANES, 2 * d), BF16),
            pltpu.VMEM((total, d), F32),
            pltpu.VMEM((total, d), BF16),
            pltpu.VMEM((total, d), F32),
        ],
        compiler_params=params(),
        name=name,
    )(*own, *halo, *bias, mask, *weights)


def per_device(tokens, group_ids, bias_table, w_qkv, w_proj, gain_attn, w_in, w_out, gain_mlp):
    samples, lev, lat_rows, lon_cols, d = tokens.shape
    lon_count = lax.axis_size("lon")
    lat_count = lax.axis_size("lat")
    lon_at = lax.axis_index("lon").astype(jnp.int32)
    lat_at = lax.axis_index("lat").astype(jnp.int32)
    par = lax.rem(lon_at, 2)
    near_pairs = [(i, i ^ 1) for i in range(lon_count)]
    far_pairs = [(i, (i + (1 if i % 2 else -1)) % lon_count) for i in range(lon_count)]
    down_pairs = [(i, (i + 1) % lat_count) for i in range(lat_count)]
    up_pairs = [(i, (i - 1) % lat_count) for i in range(lat_count)]
    at = jnp.stack([par, lat_at, lon_at])
    wins = lat_rows // WIN_LAT + 1

    cells = jnp.transpose(tokens[0], (1, 2, 0, 3)).reshape(lat_rows * lon_cols, lev, d)
    near, far, top, bot = pack(at, cells, lat_rows)
    far_halo = lax.ppermute(far, "lon", far_pairs)
    near_halo = lax.ppermute(near, "lon", near_pairs)
    above = lax.ppermute(bot, "lat", down_pairs)
    below = lax.ppermute(top, "lat", up_pairs)
    bias_near, bias_far, mask_near, mask_far, mask_edge = prep(at, group_ids, bias_table.T, wins)
    above, below, bias_near = lax.optimization_barrier((above, below, bias_near))
    edge_near, edge_far = edge_pack(above, top, bot, below)
    halo_edge_near = lax.ppermute(edge_near, "lon", near_pairs)
    halo_edge_far = lax.ppermute(edge_far, "lon", far_pairs)
    weights = [w_qkv, w_proj, gain_attn.reshape(1, -1), w_in, w_out, gain_mlp.reshape(1, -1)]
    rows = near.shape[0]
    near, edge_near = lax.optimization_barrier((near, edge_near))
    res_near = layer("near", [near], [near_halo], [bias_near], mask_near, weights, 0, rows)
    far, res_near = lax.optimization_barrier((far, res_near))
    res_far = layer("far", [far], [far_halo], [bias_far], mask_far, weights, 0, rows)
    edge_near, res_far = lax.optimization_barrier((edge_near, res_far))
    res_edge = layer(
        "edge",
        [edge_near, edge_far],
        [halo_edge_near, halo_edge_far],
        [bias_near, bias_far],
        mask_edge,
        weights,
        32,
        80,
    )
    out = unpack(at, res_near, res_far, res_edge, lat_rows * lon_cols)
    return jnp.transpose(out.reshape(lat_rows, lon_cols, lev, d), (2, 0, 1, 3))[None]


def solution(mesh):
    in_specs = (P(None, None, "lat", "lon", None), P(), P(), P(), P(), P(), P(), P(), P())
    out_specs = P(None, None, "lat", "lon", None)
    return jax.shard_map(
        per_device, mesh=mesh, in_specs=in_specs, out_specs=out_specs, check_vma=False
    )
```

time: 99.7 us -> 51 us (0.51)
  local copies, waits for them, and re-layouts: 50.3 us -> 2.96 us
  Pallas kernels: 33.1 us -> 39 us
  waiting for transfers between devices: 5.57 us -> 0.02 us
    slice x18 -> x0, local copies, waits for them, and re-layouts: 26.4 us -> none  [the longest x13 26.1 us: expand_bias(): kinds[:, :, :, WIN_LEV - 1 - z:2 * WIN_LEV - 1 - z, SHIFT_LON - 1 - w:2 *...]
    another operation x27 -> x0, local copies, waits for them, and re-layouts: 17.1 us -> none  [the longest x25 17 us: expand_bias(): spread = jnp.stack(parts, axis=2)]
    ppermute x2, waiting for transfers between devices: 5.56 us -> 0.01 us  [the longest x1 0.01 us: per_device(): halo_edge_near = lax.ppermute(edge_near, 'lon', near_pairs)]
    pallas_call x1 -> x2, Pallas kernels: 0.82 us -> 4.32 us  [the longest x1 4.27 us: prep(): pl.pallas_call(prep_kernel, in_specs=[pl.BlockSpec(memory_space=pltpu.SME...]
    broadcast_in_dim x2 -> x0, local copies, waits for them, and re-layouts: 2.34 us -> none  [the longest x1 2.02 us: per_device(): return out[None]]
    pallas_call x1, Pallas kernels: 0.54 us -> 2.54 us  [unpack(): pl.pallas_call(unpack_kernel, in_specs=[pl.BlockSpec(memory_space=pltpu.S...]
    ppermute x1, starting transfers between devices: 1.61 us -> 3.56 us  [per_device(): far_halo = lax.ppermute(far, 'lon', far_pairs)]
    squeeze x4 -> x0, local copies, waits for them, and re-layouts: 1.83 us -> none  [the longest x1 0.94 us: per_device(): above[s]]
  transfers between devices with their start and end apart: 6 -> 6, of which waited for: 1 -> 0; matrix products, arithmetic and copies ran while one was open for 48% -> 0% of each run, Pallas kernels for 20% -> 55%
where the time goes in v1:
time: 51 us; the launch traced here: 50.8 us
  Pallas kernels  39 us (76%)
  starting transfers between devices  8.61 us (17%)
  local copies, waits for them, and re-layouts  2.96 us (6%)
    pallas_call x3, Pallas kernels, layer(): pl.pallas_call(functools.partial(layer_kernel, sides, wins, q_lo, q_rows)...  29.8 us
    pallas_call x1, Pallas kernels, prep(): pl.pallas_call(prep_kernel, in_specs=[pl.BlockSpec(memory_space=pltpu.SME...  4.27 us
    ppermute x1, starting transfers between devices, per_device(): far_halo = lax.ppermute(far, 'lon', far_pairs)  3.56 us
    unnamed x12, local copies, waits for them, and re-layouts  2.96 us
    pallas_call x1, Pallas kernels, unpack(): pl.pallas_call(unpack_kernel, in_specs=[pl.BlockSpec(memory_space=pltpu.S...  2.54 us
    pallas_call x1, Pallas kernels, pack(): pl.pallas_call(pack_kernel, in_specs=[pl.BlockSpec(memory_space=pltpu.SME...  2.31 us
    ppermute x1, starting transfers between devices, per_device(): below = lax.ppermute(top, 'lat', up_pairs)  2.25 us
    ppermute x1, starting transfers between devices, per_device(): above = lax.ppermute(bot, 'lat', down_pairs)  1.58 us
  transfers between devices with their start and end apart: 6, of which 0 were waited for; matrix products, arithmetic and copies ran while one was open for 0% of the time, Pallas kernels for 55%

profile of v1, /device:TPU:0, one launch (start us, length us, event | category | flops | bytes accessed | tf_op | source)
XLA Modules:
  0.0 50.8 jit_solution(539384590382829617)
XLA Ops:
  0.0 0.0 copy-start
  0.0 0.1 pad_add_fusion.par_ref.at_ref
  0.1 0.0 copy-start.1
  0.1 1.3 %copy-done.1 = bf16[1,2,42,12,512]{4,1,3,2,0:T(2,128)(2,1)S(1)} copy-done((bf16[1,2,42,12,512]{4,1,3,2,0:T(2,128)(2,1)S(1)}, bf16[1,2,42,12,512]{4,1,3,2,0:T(2,128)(2,1)}, u32[]{:S(2)}) %copy-start.1) | copy-done | bytes 1032216
  1.3 0.0 copy-start.4
  1.3 0.0 copy-start.5
  1.3 2.3 %pack.1 = (bf16[432,512]{1,0:T(8,128)(2,1)S(1)}, bf16[432,512]{1,0:T(8,128)(2,1)S(1)}, bf16[2,36,512]{2,1,0:T(8,128)(2,1)S(1)}, bf16[2,36,512]{2,1,0:T(8,128)(2,1)S(1)}) custom-call(s32[3]{0:T(128)S(1)} %pad_add_fusion.par_ref.at_ref, bf16[504,2,512]{2,1,0:T(2,128)(2,1)S(1)} %bitcast.16), custom_call_target="tpu_custom_call" | custom-call | tf_op jit(solution)/shard_map/pack/pallas_call | solution.py:81
  3.7 0.5 %collective-permute-start.2 = (bf16[432,512]{1,0:T(8,128)(2,1)S(1)}, bf16[432,512]{1,0:T(8,128)(2,1)S(1)}, u32[]{:S(2)}, u32[]{:S(2)}) collective-permute-start(bf16[432,512]{1,0:T(8,128)(2,1)S(1)} %get-tuple-element.33.refs_0_), channel_id=1, source_target_pairs={{0,4},{4,0},{8,12},{12,8},{16,20},{20,16},{24,28},{28,24},{1,5},{5... | collective-permute-start | bytes 1327112 | tf_op jit(solution)/shard_map/ppermute | solution.py:413
  4.2 3.6 %collective-permute-start.3 = (bf16[432,512]{1,0:T(8,128)(2,1)S(1)}, bf16[432,512]{1,0:T(8,128)(2,1)S(1)}, u32[]{:S(2)}, u32[]{:S(2)}) collective-permute-start(bf16[432,512]{1,0:T(8,128)(2,1)S(1)} %get-tuple-element.38.refs_0_), channel_id=1, source_target_pairs={{0,28},{4,8},{8,4},{12,16},{16,12},{20,24},{24,20},{28,0},{1,29},{... | collective-permute-start | bytes 1327112 | tf_op jit(solution)/shard_map/ppermute | solution.py:412
  7.7 1.6 %collective-permute-start = (bf16[2,36,512]{2,1,0:T(8,128)(2,1)S(1)}, bf16[2,36,512]{2,1,0:T(8,128)(2,1)S(1)}, u32[]{:S(2)}, u32[]{:S(2)}) collective-permute-start(bf16[2,36,512]{2,1,0:T(8,128)(2,1)S(1)} %get-tuple-element.27.bot_ref), channel_id=1, source_target_pairs={{0,1},{1,2},{2,3},{3,0},{4,5},{5,6},{6,7},{7,4},{8,9},{9,10},{10,1... | collective-permute-start | bytes 221192 | tf_op jit(solution)/shard_map/ppermute | solution.py:414
  9.3 2.2 %collective-permute-start.1 = (bf16[2,36,512]{2,1,0:T(8,128)(2,1)S(1)}, bf16[2,36,512]{2,1,0:T(8,128)(2,1)S(1)}, u32[]{:S(2)}, u32[]{:S(2)}) collective-permute-start(bf16[2,36,512]{2,1,0:T(8,128)(2,1)S(1)} %get-tuple-element.28.top_ref), channel_id=1, source_target_pairs={{0,3},{1,0},{2,1},{3,2},{4,7},{5,4},{6,5},{7,6},{8,11},{9,8},{10,9... | collective-permute-start | bytes 221192 | tf_op jit(solution)/shard_map/ppermute | solution.py:415
  11.6 0.0 copy-start.2
  11.6 0.9 %copy-done.2 = s32[168,96]{1,0:T(8,128)S(1)} copy-done((s32[168,96]{1,0:T(8,128)S(1)}, s32[168,96]{1,0:T(8,128)}, u32[]{:S(2)}) %copy-start.2) | copy-done | bytes 64536
  12.5 0.0 copy-start.3
  12.5 0.8 %copy-done.3 = f32[759,16]{0,1:T(8,128)S(1)} copy-done((f32[759,16]{0,1:T(8,128)S(1)}, f32[759,16]{0,1:T(8,128)}, u32[]{:S(2)}) %copy-start.3) | copy-done | bytes 48600
  13.3 4.3 %prep.1 = (f32[16,72,256]{2,1,0:T(8,128)S(1)}, f32[16,72,256]{2,1,0:T(8,128)S(1)}, f32[6,72,256]{2,1,0:T(8,128)S(1)}, f32[6,72,256]{2,1,0:T(8,128)S(1)}, f32[4,72,256]{2,1,0:T(8,128)S(1)}) custom-call(s32[3]{0:T(128)S(1)} %pad_add_fusion.par_ref.at_ref, s32[168,96]{1,0:T(8,128)S(1)} %copy-done.2, f32[16,759]{1,0:T(8,128)S(1)} %bitcast.17, ...), custom_call_target="tpu_custom_call" | custom-call | tf_op jit(solution)/shard_map/prep/pallas_call | solution.py:239
  17.5 0.0 collective-permute-done.above_ref
  17.5 0.0 collective-permute-done.1.below_ref
  17.5 0.1 edge_pack.1
  17.6 0.1 collective-permute-start.4
  17.7 0.6 %collective-permute-start.5 = (bf16[144,512]{1,0:T(8,128)(2,1)S(1)}, bf16[144,512]{1,0:T(8,128)(2,1)S(1)}, u32[]{:S(2)}, u32[]{:S(2)}) collective-permute-start(bf16[144,512]{1,0:T(8,128)(2,1)S(1)} %get-tuple-element.43.refs_1_), channel_id=1, source_target_pairs={{0,28},{4,8},{8,4},{12,16},{16,12},{20,24},{24,20},{28,0},{1,29},{... | collective-permute-start | bytes 442376 | tf_op jit(solution)/shard_map/ppermute | solution.py:420
  18.3 0.0 collective-permute-done.2.refs_1_
  18.3 0.0 copy-done
  18.3 0.0 copy-done.4
  18.3 0.0 copy-done.5
  18.3 11.8 %near.1.near_ref = bf16[432,512]{1,0:T(8,128)(2,1)S(1)} custom-call(bf16[432,512]{1,0:T(8,128)(2,1)S(1)} %get-tuple-element.33.refs_0_, bf16[432,512]{1,0:T(8,128)(2,1)S(1)} %collective-permute-done.2.refs_1_, f32[16,72,256]{2,1,0:T(8,128)S(1)} %get-tuple-element.34.refs_2_.refs_4_, f32[6,72,256]{2,1,0:T(8,128)S(1)} %get-tuple-element.35.refs_3_, ...), custom_call_target="tpu_custom_call" | custom-call | tf_op jit(solution)/shard_map/near/pallas_call | solution.py:378
  30.1 0.0 collective-permute-done.3.refs_1_
  30.1 11.6 %far.1.far_ref = bf16[432,512]{1,0:T(8,128)(2,1)S(1)} custom-call(bf16[432,512]{1,0:T(8,128)(2,1)S(1)} %get-tuple-element.38.refs_0_, bf16[432,512]{1,0:T(8,128)(2,1)S(1)} %collective-permute-done.3.refs_1_, f32[16,72,256]{2,1,0:T(8,128)S(1)} %get-tuple-element.39.refs_2_.refs_5_, f32[6,72,256]{2,1,0:T(8,128)S(1)} %get-tuple-element.40.refs_3_, ...), custom_call_target="tpu_custom_call" | custom-call | tf_op jit(solution)/shard_map/far/pallas_call | solution.py:378
  41.7 0.0 collective-permute-done.4.refs_2_
  41.8 0.0 collective-permute-done.5.refs_3_
  41.8 6.4 %edge.1.edge_ref = bf16[2,80,512]{2,1,0:T(8,128)(2,1)S(1)} custom-call(bf16[144,512]{1,0:T(8,128)(2,1)S(1)} %get-tuple-element.42.refs_0_, bf16[144,512]{1,0:T(8,128)(2,1)S(1)} %get-tuple-element.43.refs_1_, bf16[144,512]{1,0:T(8,128)(2,1)S(1)} %collective-permute-done.4.refs_2_, bf16[144,512]{1,0:T(8,128)(2,1)S(1)} %collective-permute-done.5.refs_3_, ...), custom_call_target="tpu_custom_call" | custom-call | tf_op jit(solution)/shard_map/edge/pallas_call | solution.py:378
  48.2 2.5 %unpack.1 = bf16[504,2,512]{2,1,0:T(2,128)(2,1)} custom-call(s32[3]{0:T(128)S(1)} %pad_add_fusion.par_ref.at_ref, bf16[432,512]{1,0:T(8,128)(2,1)S(1)} %near.1.near_ref, bf16[432,512]{1,0:T(8,128)(2,1)S(1)} %far.1.far_ref, bf16[2,80,512]{2,1,0:T(8,128)(2,1)S(1)} %edge.1.edge_ref), custom_call_target="tpu_custom_call" | custom-call | tf_op jit(solution)/shard_map/unpack/pallas_call | solution.py:144
Async XLA Ops:
  0.0 18.3 %copy-start = (bf16[512,512]{1,0:T(8,128)(2,1)S(1)}, bf16[512,512]{1,0:T(8,128)(2,1)}, u32[]{:S(2)}) copy-start(bf16[512,512]{1,0:T(8,128)(2,1)} %refs_8_.5) | copy-start | bytes 1572868
  0.1 1.3 %copy-start.1 = (bf16[1,2,42,12,512]{4,1,3,2,0:T(2,128)(2,1)S(1)}, bf16[1,2,42,12,512]{4,1,3,2,0:T(2,128)(2,1)}, u32[]{:S(2)}) copy-start(bf16[1,2,42,12,512]{4,1,3,2,0:T(2,128)(2,1)} %param.10) | copy-start | bytes 3096580
  1.3 17.0 %copy-start.4 = (f32[512]{0:T(512)S(1)}, f32[512]{0:T(512)}, u32[]{:S(2)}) copy-start(f32[512]{0:T(512)} %param.15) | copy-start | bytes 6148
  1.3 17.0 %copy-start.5 = (f32[512]{0:T(512)S(1)}, f32[512]{0:T(512)}, u32[]{:S(2)}) copy-start(f32[512]{0:T(512)} %param.18) | copy-start | bytes 6148
  3.7 14.7 %collective-permute-start.2 = (bf16[432,512]{1,0:T(8,128)(2,1)S(1)}, bf16[432,512]{1,0:T(8,128)(2,1)S(1)}, u32[]{:S(2)}, u32[]{:S(2)}) collective-permute-start(bf16[432,512]{1,0:T(8,128)(2,1)S(1)} %get-tuple-element.33.refs_0_), channel_id=1, source_target_pairs={{0,4},{4,0},{8,12},{12,8},{16,20},{20,16},{24,28},{28,24},{1,5},{5... | collective-permute-start | bytes 1327112 | tf_op jit(solution)/shard_map/ppermute | solution.py:413
  4.2 26.0 %collective-permute-start.3 = (bf16[432,512]{1,0:T(8,128)(2,1)S(1)}, bf16[432,512]{1,0:T(8,128)(2,1)S(1)}, u32[]{:S(2)}, u32[]{:S(2)}) collective-permute-start(bf16[432,512]{1,0:T(8,128)(2,1)S(1)} %get-tuple-element.38.refs_0_), channel_id=1, source_target_pairs={{0,28},{4,8},{8,4},{12,16},{16,12},{20,24},{24,20},{28,0},{1,29},{... | collective-permute-start | bytes 1327112 | tf_op jit(solution)/shard_map/ppermute | solution.py:412
  7.7 9.8 %collective-permute-start = (bf16[2,36,512]{2,1,0:T(8,128)(2,1)S(1)}, bf16[2,36,512]{2,1,0:T(8,128)(2,1)S(1)}, u32[]{:S(2)}, u32[]{:S(2)}) collective-permute-start(bf16[2,36,512]{2,1,0:T(8,128)(2,1)S(1)} %get-tuple-element.27.bot_ref), channel_id=1, source_target_pairs={{0,1},{1,2},{2,3},{3,0},{4,5},{5,6},{6,7},{7,4},{8,9},{9,10},{10,1... | collective-permute-start | bytes 221192 | tf_op jit(solution)/shard_map/ppermute | solution.py:414
  9.3 8.2 %collective-permute-start.1 = (bf16[2,36,512]{2,1,0:T(8,128)(2,1)S(1)}, bf16[2,36,512]{2,1,0:T(8,128)(2,1)S(1)}, u32[]{:S(2)}, u32[]{:S(2)}) collective-permute-start(bf16[2,36,512]{2,1,0:T(8,128)(2,1)S(1)} %get-tuple-element.28.top_ref), channel_id=1, source_target_pairs={{0,3},{1,0},{2,1},{3,2},{4,7},{5,4},{6,5},{7,6},{8,11},{9,8},{10,9... | collective-permute-start | bytes 221192 | tf_op jit(solution)/shard_map/ppermute | solution.py:415
  11.6 0.9 %copy-start.2 = (s32[168,96]{1,0:T(8,128)S(1)}, s32[168,96]{1,0:T(8,128)}, u32[]{:S(2)}) copy-start(s32[168,96]{1,0:T(8,128)} %gid_ref.1) | copy-start | bytes 193540
  12.5 0.8 %copy-start.3 = (f32[759,16]{0,1:T(8,128)S(1)}, f32[759,16]{0,1:T(8,128)}, u32[]{:S(2)}) copy-start(f32[759,16]{0,1:T(8,128)} %param.12) | copy-start | bytes 145732
  17.6 24.1 %collective-permute-start.4 = (bf16[144,512]{1,0:T(8,128)(2,1)S(1)}, bf16[144,512]{1,0:T(8,128)(2,1)S(1)}, u32[]{:S(2)}, u32[]{:S(2)}) collective-permute-start(bf16[144,512]{1,0:T(8,128)(2,1)S(1)} %get-tuple-element.42.refs_0_), channel_id=1, source_target_pairs={{0,4},{4,0},{8,12},{12,8},{16,20},{20,16},{24,28},{28,24},{1,5},{5... | collective-permute-start | bytes 442376 | tf_op jit(solution)/shard_map/ppermute | solution.py:419
  17.7 24.1 %collective-permute-start.5 = (bf16[144,512]{1,0:T(8,128)(2,1)S(1)}, bf16[144,512]{1,0:T(8,128)(2,1)S(1)}, u32[]{:S(2)}, u32[]{:S(2)}) collective-permute-start(bf16[144,512]{1,0:T(8,128)(2,1)S(1)} %get-tuple-element.43.refs_1_), channel_id=1, source_target_pairs={{0,28},{4,8},{8,4},{12,16},{16,12},{20,24},{24,20},{28,0},{1,29},{... | collective-permute-start | bytes 442376 | tf_op jit(solution)/shard_map/ppermute | solution.py:420

commit v2 on v1

v2 whole, which is shorter than its diff:
```python
import functools

import jax
import jax.numpy as jnp
import numpy as np
from jax import lax
from jax.experimental import pallas as pl
from jax.experimental.pallas import tpu as pltpu
from jax.sharding import PartitionSpec as P

WIN_LEV = 2
WIN_LAT = 6
WIN_LON = 12
SHIFT_LAT = 3
SHIFT_LON = 6

EPS = 1e-05
LOG2E = 1.4426950408889634
HALF = WIN_LEV * WIN_LAT * SHIFT_LON
ROW = WIN_LEV * SHIFT_LON
EDGE = SHIFT_LAT * ROW
KEYS = 2 * HALF
SPREAD = 256
GROUP = 4
VMEM_LIMIT = 24 * 1024 * 1024
PACK_LIMIT = 20 * 1024 * 1024

F32 = jnp.float32
BF16 = jnp.bfloat16


def params(limit=VMEM_LIMIT):
    return pltpu.CompilerParams(vmem_limit_bytes=limit)


def cost(micros):
    return pl.CostEstimate(flops=int(micros * 1e9), bytes_accessed=int(micros * 3e6), transcendentals=0)


def anywhere(count):
    return [pl.BlockSpec(memory_space=pl.ANY)] * count


def vmem(count):
    return [pl.BlockSpec(memory_space=pltpu.VMEM)] * count


def pack_kernel(par_ref, tok_ref, near_ref, far_ref, top_ref, bot_ref):
    lat, d = tok_ref.shape[0], tok_ref.shape[-1]
    par = par_ref[0]
    for side, out in ((1, far_ref), (0, near_ref)):
        half = par if side else 1 - par
        out[...] = tok_ref[SHIFT_LAT : lat - SHIFT_LAT, half].reshape(out.shape)
        top_ref[side] = tok_ref[:SHIFT_LAT, half].reshape(EDGE, d)
        bot_ref[side] = tok_ref[lat - SHIFT_LAT :, half].reshape(EDGE, d)


def pack(par, cells):
    lat, _, lon, lev, d = cells.shape
    main = (lat - 2 * SHIFT_LAT) * ROW
    return pl.pallas_call(
        pack_kernel,
        in_specs=[pl.BlockSpec(memory_space=pltpu.SMEM)] + vmem(1),
        out_specs=vmem(4),
        out_shape=[
            jax.ShapeDtypeStruct((main, d), BF16),
            jax.ShapeDtypeStruct((main, d), BF16),
            jax.ShapeDtypeStruct((2, EDGE, d), BF16),
            jax.ShapeDtypeStruct((2, EDGE, d), BF16),
        ],
        compiler_params=params(PACK_LIMIT),
        cost_estimate=cost(1),
        name="pack",
    )(par, cells)


def edge_pack_kernel(above_ref, top_ref, bot_ref, below_ref, near_ref, far_ref, scr):
    for side, out in enumerate((near_ref, far_ref)):
        for i, ref in enumerate((above_ref, top_ref, bot_ref, below_ref)):
            scr[i * EDGE : (i + 1) * EDGE, :] = ref[side].astype(F32)
        out[...] = scr[...].astype(BF16)


def edge_pack(above, top, bot, below):
    d = top.shape[2]
    return pl.pallas_call(
        edge_pack_kernel,
        in_specs=vmem(4),
        out_specs=vmem(2),
        out_shape=[jax.ShapeDtypeStruct((4 * EDGE, d), BF16)] * 2,
        scratch_shapes=[pltpu.VMEM((4 * EDGE, d), F32)],
        compiler_params=params(),
        name="edge_pack",
    )(above, top, bot, below)


def spread_matrix(count):
    nw, nh = 2 * WIN_LON - 1, 2 * WIN_LAT - 1
    out = np.zeros((count, 3, SPREAD), np.float32)
    for kind, centre in enumerate((WIN_LON - 1, SHIFT_LON - 1, WIN_LON + SHIFT_LON - 1)):
        for j in range(nh):
            for w in range(SHIFT_LON):
                for z in range(WIN_LEV):
                    at = (WIN_LEV - 1 - z) * nh * nw + (nh - 1 - j) * nw + centre - w
                    out[at, kind, j * ROW + w * WIN_LEV + z] = 1
    return out.reshape(count, 3 * SPREAD)


def prep_kernel(
    at_ref,
    gid_any,
    table_any,
    spread_any,
    bias_near,
    bias_far,
    mask_near,
    mask_far,
    mask_edge,
    wide,
    kinds,
    gid_ref,
    table_ref,
    spread_ref,
    sems,
):
    pairs = ((table_any, table_ref), (gid_any, gid_ref), (spread_any, spread_ref))
    copies = [pltpu.make_async_copy(src, dst, sems.at[i]) for i, (src, dst) in enumerate(pairs)]
    for copy in copies:
        copy.start()
    heads, offsets = table_ref.shape
    nw, nh = 2 * WIN_LON - 1, 2 * WIN_LAT - 1
    par, lat_at, lon_at = at_ref[0], at_ref[1], at_ref[2]
    count = wide.shape[1]
    wide[...] = jnp.zeros_like(wide)
    copies[0].wait()
    wide[:, :offsets] = table_ref[...] * LOG2E
    x = jnp.broadcast_to(wide[...][:, None, :], (heads, 16, count)).reshape(heads * 16, count)
    place = lax.broadcasted_iota(jnp.int32, x.shape, 0) % 16
    for amount, bit in ((nh * nw, place % 2), (1, place // 2 % 2), (2, place // 4 % 2), (4, place // 8)):
        x = jnp.where(bit == 1, pltpu.roll(x, count - amount, 1), x)
    high = x.astype(BF16)
    low = (x - high.astype(F32)).astype(BF16)
    copies[2].wait()
    for kind in range(3):
        m = spread_ref[:, kind * SPREAD : (kind + 1) * SPREAD]
        y = jnp.dot(high, m, preferred_element_type=F32) + jnp.dot(low, m, preferred_element_type=F32)
        kinds[kind] = y.reshape(heads, 16, SPREAD)
    for side, out in enumerate((bias_near, bias_far)):
        halo = kinds[2 - par if side else 1 + par]
        for h in range(WIN_LAT):
            start = (WIN_LAT - 1 - h) * ROW
            out[:, h * ROW : (h + 1) * ROW, :HALF] = kinds[0, :, :ROW, start : start + HALF]
            out[:, h * ROW : (h + 1) * ROW, HALF:KEYS] = halo[:, :ROW, start : start + HALF]
    copies[1].wait()
    total, around = gid_ref.shape
    wins = mask_near.shape[0] + 2
    lat_rows = (wins - 1) * WIN_LAT
    lane = lax.broadcasted_iota(jnp.int32, (1, KEYS), 1)
    is_halo = lane >= HALF
    rest = jnp.where(is_halo, lane - HALF, lane)
    h_of = rest // ROW
    w_of = rest % ROW // WIN_LEV
    ids = gid_ref[...].astype(BF16)
    row = lax.broadcasted_iota(jnp.int32, (total, KEYS), 0)
    col = lax.broadcasted_iota(jnp.int32, (around, KEYS), 0)
    for side in range(2):
        right = par == side
        offset = jnp.where(
            right, jnp.where(is_halo, SHIFT_LON, 0), jnp.where(is_halo, -WIN_LON, -SHIFT_LON)
        )
        want = lon_at * 2 * SHIFT_LON + offset + w_of
        want = jnp.where(want < 0, want + around, want)
        pick = jnp.where(col == want, 1.0, 0.0).astype(BF16)
        label = 2.0 * jnp.dot(ids, pick, preferred_element_type=F32)
        label = label + jnp.where(row >= total - SHIFT_LAT, 1.0, 0.0)
        lines = []
        for k in range(wins):
            want = lat_at * lat_rows + (k - 1) * WIN_LAT + h_of
            want = jnp.where(want < 0, want + total, want)
            line = jnp.sum(jnp.where(row == want, label, 0.0), 0, keepdims=True)
            lines.append(line)
        lines = jnp.concatenate(lines, 0)
        cols = lines[:, :128].T
        for k in range(wins):
            same = cols[:HALF, k : k + 1] == lines[k : k + 1, :]
            mask = jnp.where(same, 0.0, -jnp.inf)
            if k == 0:
                mask_edge[2 * side] = mask
            elif k == wins - 1:
                mask_edge[2 * side + 1] = mask
            elif side == 0:
                mask_near[k - 1] = mask
            else:
                mask_far[k - 1] = mask


def prep(at, group_ids, table, wins):
    heads, offsets = table.shape
    count = -(-offsets // 256) * 256
    spread = jnp.asarray(spread_matrix(count), BF16)
    return pl.pallas_call(
        prep_kernel,
        in_specs=[pl.BlockSpec(memory_space=pltpu.SMEM)] + anywhere(3),
        out_specs=vmem(5),
        out_shape=[jax.ShapeDtypeStruct((heads, HALF, KEYS), F32)] * 2
        + [jax.ShapeDtypeStruct((wins - 2, HALF, KEYS), F32)] * 2
        + [jax.ShapeDtypeStruct((4, HALF, KEYS), F32)],
        scratch_shapes=[
            pltpu.VMEM((heads, count), F32),
            pltpu.VMEM((3, heads, 16, SPREAD), F32),
            pltpu.VMEM(group_ids.shape, jnp.int32),
            pltpu.VMEM(table.shape, F32),
            pltpu.VMEM(spread.shape, BF16),
            pltpu.SemaphoreType.DMA((3,)),
        ],
        compiler_params=params(),
        cost_estimate=cost(5),
        name="prep",
    )(at, group_ids, table, spread)


def norm_rows(value, gain):
    mean = jnp.mean(value, -1, keepdims=True)
    centred = value - mean
    var = jnp.mean(centred * centred, -1, keepdims=True)
    return centred * lax.rsqrt(var + EPS) * gain


def gelu(x):
    return 0.5 * x * (1.0 + lax.erf(x * 0.7071067811865476))


def attend(q, k, v, extra, mask, lane_head, hd):
    per, lanes = q.shape
    lhs = jnp.concatenate([jnp.where(lane_head == j, q, 0.0) for j in range(GROUP)], 0).astype(BF16)
    sc = lax.dot_general(lhs, k, (((1,), (1,)), ((), ())), preferred_element_type=F32)
    sc = sc + extra.reshape(GROUP * per, KEYS) + mask
    top = jnp.max(sc, -1, keepdims=True)
    p = jnp.exp2(sc - top).astype(BF16)
    o = jnp.dot(p, v, preferred_element_type=F32)
    num, den = o[:per, :lanes], o[:per, lanes:]
    for j in range(1, GROUP):
        here = lane_head == j
        num = jnp.where(here, o[j * per : (j + 1) * per, :lanes], num)
        den = jnp.where(here, o[j * per : (j + 1) * per, lanes:], den)
    return num / den


def layer_body(blocks, weights, scratch):
    w_qkv, w_proj, w_in, w_out, gain_attn, gain_mlp = weights
    q_scr, k_scr, v_scr, o_scr, mid_scr, acc_scr = scratch
    d = w_proj.shape[0]
    heads = blocks[0][2].shape[0]
    hd = d // heads
    lanes = GROUP * hd
    groups = heads // GROUP
    scale = LOG2E / hd**0.5
    step = 2 * lanes
    wi = 0
    for g in range(groups):
        ones = jnp.ones((v_scr.shape[0], KEYS, lanes), BF16)
        v_scr[:, :, (2 * g + 1) * lanes : (2 * g + 2) * lanes] = ones
    base = 0
    for own, halo, bias, mask_ref, mask_at, q_lo, q_rows in blocks:
        wins = own.shape[0] // HALF
        per = q_rows // wins
        for c in range(0, d, step):
            q = jnp.dot(own[q_lo : q_lo + q_rows, :], w_qkv[:, c : c + step], preferred_element_type=F32)
            q_scr[base : base + q_rows, c : c + step] = q * scale
            for part in (d, 2 * d):
                w = w_qkv[:, part + c : part + c + step]
                a = jnp.dot(own[...], w, preferred_element_type=F32)
                b = jnp.dot(halo[...], w, preferred_element_type=F32)
                for i in range(wins):
                    both = jnp.concatenate(
                        [a[i * HALF : (i + 1) * HALF], b[i * HALF : (i + 1) * HALF]], 0
                    ).astype(BF16)
                    if part == d:
                        k_scr[wi + i, :, c : c + step] = both
                    else:
                        v_scr[wi + i, :, 2 * c : 2 * c + lanes] = both[:, :lanes]
                        v_scr[wi + i, :, 2 * c + step : 2 * c + step + lanes] = both[:, lanes:]
        lane_head = lax.broadcasted_iota(jnp.int32, (per, lanes), 1) // hd
        for i in range(wins):
            first = q_lo + i * per - i * HALF
            at = base + i * per
            mask = jnp.concatenate([mask_ref[mask_at + i, first : first + per, :]] * GROUP, 0)
            for g in range(groups):
                o_scr[at : at + per, g * lanes : (g + 1) * lanes] = attend(
                    q_scr[at : at + per, g * lanes : (g + 1) * lanes],
                    k_scr[wi + i, :, g * lanes : (g + 1) * lanes],
                    v_scr[wi + i, :, 2 * g * lanes : (2 * g + 2) * lanes],
                    bias[g * GROUP : (g + 1) * GROUP, first : first + per, :],
                    mask,
                    lane_head,
                    hd,
                )
        base += q_rows
        wi += wins
    proj = jnp.dot(o_scr[...].astype(BF16), w_proj[...], preferred_element_type=F32)
    branch = norm_rows(proj, gain_attn[...]).astype(BF16).astype(F32)
    base = 0
    for own, _, _, _, _, q_lo, q_rows in blocks:
        mid_scr[base : base + q_rows, :] = (
            own[q_lo : q_lo + q_rows, :].astype(F32) + branch[base : base + q_rows]
        ).astype(BF16)
        base += q_rows
    ff = w_in.shape[1]
    chunk = 256
    for c in range(0, ff, chunk):
        up = jnp.dot(mid_scr[...], w_in[:, c : c + chunk], preferred_element_type=F32)
        hid = gelu(up).astype(BF16)
        down = jnp.dot(hid, w_out[c : c + chunk, :], preferred_element_type=F32)
        if c == 0:
            acc_scr[...] = down
        else:
            acc_scr[...] += down
    return mid_scr[...].astype(F32) + norm_rows(acc_scr[...], gain_mlp[...])


def near_kernel(own, halo, bias, mask, *refs):
    weights, out, scratch = refs[:6], refs[6], refs[7:]
    rows, d = own.shape
    res = layer_body([(own, halo, bias, mask, 0, 0, rows)], weights, scratch)
    out[...] = res.reshape(out.shape).astype(BF16)


def last_kernel(
    par_ref, near_res, far, far_halo, e_near, e_near_halo, e_far, e_far_halo, *refs
):
    bias_near, bias_far, mask_far, mask_edge = refs[:4]
    weights, out, near_sem, sems, far_buf, edge_buf = refs[4:10], *refs[10:15]
    scratch = refs[15:]
    par = par_ref[0]
    lat = out.shape[0]
    halves = (1 - par, par)
    main = pl.ds(SHIFT_LAT, lat - 2 * SHIFT_LAT)
    first = pltpu.make_async_copy(near_res, out.at[main, halves[0]], near_sem)
    first.start()
    rows = far.shape[0]
    lo, keep = EDGE // 8 * 8, 80
    res = layer_body(
        [
            (far, far_halo, bias_far, mask_far, 0, 0, rows),
            (e_near, e_near_halo, bias_near, mask_edge, 0, lo, keep),
            (e_far, e_far_halo, bias_far, mask_edge, 2, lo, keep),
        ],
        weights,
        scratch,
    )
    far_buf[...] = res[:rows].reshape(far_buf.shape).astype(BF16)
    copies = [pltpu.make_async_copy(far_buf, out.at[main, halves[1]], sems.at[4])]
    copies[0].start()
    shape = edge_buf.shape[2:]
    for side in range(2):
        at = rows + side * keep + EDGE - lo
        for end in range(2):
            part = res[at + end * EDGE : at + (end + 1) * EDGE]
            edge_buf[side, end] = part.reshape(shape).astype(BF16)
            place = pl.ds(end * (lat - SHIFT_LAT), SHIFT_LAT)
            copies.append(
                pltpu.make_async_copy(
                    edge_buf.at[side, end], out.at[place, halves[side]], sems.at[2 * side + end]
                )
            )
            copies[-1].start()
    for copy in copies:
        copy.wait()
    first.wait()


def layer_scratch(total, windows, weights):
    d = weights[1].shape[0]
    return [
        pltpu.VMEM((total, d), F32),
        pltpu.VMEM((windows, KEYS, d), BF16),
        pltpu.VMEM((windows, KEYS, 2 * d), BF16),
        pltpu.VMEM((total, d), F32),
        pltpu.VMEM((total, d), BF16),
        pltpu.VMEM((total, d), F32),
    ]


def near_layer(own, halo, bias, mask, weights):
    rows, d = own.shape
    shape = (rows // ROW, SHIFT_LON, WIN_LEV, d)
    return pl.pallas_call(
        near_kernel,
        in_specs=vmem(10),
        out_specs=vmem(1)[0],
        out_shape=jax.ShapeDtypeStruct(shape, BF16),
        scratch_shapes=layer_scratch(rows, rows // HALF, weights),
        compiler_params=params(),
        cost_estimate=cost(8),
        name="near",
    )(own, halo, bias, mask, *weights)


def last_layer(par, near_res, far, far_halo, edges, bias, masks, weights):
    rows, d = far.shape
    lat = rows // ROW + 2 * SHIFT_LAT
    shape = (lat, 2, SHIFT_LON, WIN_LEV, d)
    return pl.pallas_call(
        last_kernel,
        in_specs=[pl.BlockSpec(memory_space=pltpu.SMEM)] + vmem(17),
        out_specs=pl.BlockSpec(memory_space=pl.ANY),
        out_shape=jax.ShapeDtypeStruct(shape, BF16),
        scratch_shapes=[
            pltpu.SemaphoreType.DMA,
            pltpu.SemaphoreType.DMA((5,)),
            pltpu.VMEM((rows // ROW, SHIFT_LON, WIN_LEV, d), BF16),
            pltpu.VMEM((2, 2, SHIFT_LAT, SHIFT_LON, WIN_LEV, d), BF16),
        ]
        + layer_scratch(rows + 160, rows // HALF + 4, weights),
        compiler_params=params(),
        cost_estimate=cost(12),
        name="last",
    )(par, near_res, far, far_halo, *edges, *bias, *masks, *weights)


def per_device(tokens, group_ids, bias_table, w_qkv, w_proj, gain_attn, w_in, w_out, gain_mlp):
    samples, lev, lat_rows, lon_cols, d = tokens.shape
    lon_count = lax.axis_size("lon")
    lat_count = lax.axis_size("lat")
    lon_at = lax.axis_index("lon").astype(jnp.int32)
    lat_at = lax.axis_index("lat").astype(jnp.int32)
    par = lax.rem(lon_at, 2)
    near_pairs = [(i, i ^ 1) for i in range(lon_count)]
    far_pairs = [(i, (i + (1 if i % 2 else -1)) % lon_count) for i in range(lon_count)]
    down_pairs = [(i, (i + 1) % lat_count) for i in range(lat_count)]
    up_pairs = [(i, (i - 1) % lat_count) for i in range(lat_count)]
    at = jnp.stack([par, lat_at, lon_at])
    wins = lat_rows // WIN_LAT + 1

    cells = jnp.transpose(tokens[0], (1, 2, 0, 3)).reshape(lat_rows, 2, SHIFT_LON, lev, d)
    near, far, top, bot = pack(at, cells)
    far_halo = lax.ppermute(far, "lon", far_pairs)
    near_halo = lax.ppermute(near, "lon", near_pairs)
    above = lax.ppermute(bot, "lat", down_pairs)
    below = lax.ppermute(top, "lat", up_pairs)
    bias_near, bias_far, mask_near, mask_far, mask_edge = prep(at, group_ids, bias_table.T, wins)
    above, below, bias_near = lax.optimization_barrier((above, below, bias_near))
    edge_near, edge_far = edge_pack(above, top, bot, below)
    edge_near_halo = lax.ppermute(edge_near, "lon", near_pairs)
    edge_far_halo = lax.ppermute(edge_far, "lon", far_pairs)
    weights = [w_qkv, w_proj, w_in, w_out, gain_attn.reshape(1, -1), gain_mlp.reshape(1, -1)]
    near, edge_near = lax.optimization_barrier((near, edge_near))
    near_res = near_layer(near, near_halo, bias_near, mask_near, weights)
    out = last_layer(
        at,
        near_res,
        far,
        far_halo,
        [edge_near, edge_near_halo, edge_far, edge_far_halo],
        [bias_near, bias_far],
        [mask_far, mask_edge],
        weights,
    )
    return jnp.transpose(out.reshape(lat_rows, lon_cols, lev, d), (2, 0, 1, 3))[None]


def solution(mesh):
    in_specs = (P(None, None, "lat", "lon", None), P(), P(), P(), P(), P(), P(), P(), P())
    out_specs = P(None, None, "lat", "lon", None)
    return jax.shard_map(
        per_device, mesh=mesh, in_specs=in_specs, out_specs=out_specs, check_vma=False
    )
```

time: 51 us -> 34.7 us (0.68)
  Pallas kernels: 39 us -> 23.2 us
  local copies, waits for them, and re-layouts: 2.96 us -> 1.27 us
  waiting for transfers between devices: 0.02 us -> 1.04 us
    pallas_call x4 -> x2, Pallas kernels: 32.4 us -> 18.3 us  [the longest x1 11.4 us: last_layer(): pl.pallas_call(last_kernel, in_specs=[pl.BlockSpec(memory_space=pltpu.SME...]
    unnamed x12 -> x20, local copies, waits for them, and re-layouts: 2.96 us -> 1.27 us
    pallas_call x1, Pallas kernels: 2.31 us -> 0.67 us  [pack(): pl.pallas_call(pack_kernel, in_specs=[pl.BlockSpec(memory_space=pltpu.SME...]
    ppermute x1, starting transfers between devices: 1.58 us -> 3.08 us  [per_device(): above = lax.ppermute(bot, 'lat', down_pairs)]
    ppermute x2, waiting for transfers between devices: 0.01 us -> 1.03 us  [the longest x1 1.03 us: per_device(): edge_far_halo = lax.ppermute(edge_far, 'lon', far_pairs)]
    ppermute x1, starting transfers between devices: 3.56 us -> 2.72 us  [per_device(): far_halo = lax.ppermute(far, 'lon', far_pairs)]
    ppermute x1, starting transfers between devices: 0.52 us -> 0.01 us  [per_device(): near_halo = lax.ppermute(near, 'lon', near_pairs)]
  transfers between devices with their start and end apart: 6 -> 6, of which waited for: 0 -> 1; matrix products, arithmetic and copies ran while one was open for 0% -> 0% of each run, Pallas kernels for 55% -> 32%
where the time goes in v2:
time: 34.7 us; the launch traced here: 34.5 us
  Pallas kernels  23.2 us (67%)
  starting transfers between devices  8.59 us (25%)
  local copies, waits for them, and re-layouts  1.27 us (4%)
  waiting for transfers between devices  1.04 us (3%)
    pallas_call x1, Pallas kernels, last_layer(): pl.pallas_call(last_kernel, in_specs=[pl.BlockSpec(memory_space=pltpu.SME...  11.4 us
    pallas_call x1, Pallas kernels, near_layer(): pl.pallas_call(near_kernel, in_specs=vmem(10), out_specs=vmem(1)[0], out_...  6.94 us
    pallas_call x1, Pallas kernels, prep(): pl.pallas_call(prep_kernel, in_specs=[pl.BlockSpec(memory_space=pltpu.SME...  4.17 us
    ppermute x1, starting transfers between devices, per_device(): above = lax.ppermute(bot, 'lat', down_pairs)  3.08 us
    ppermute x1, starting transfers between devices, per_device(): far_halo = lax.ppermute(far, 'lon', far_pairs)  2.72 us
    ppermute x1, starting transfers between devices, per_device(): below = lax.ppermute(top, 'lat', up_pairs)  2.09 us
    unnamed x20, local copies, waits for them, and re-layouts  1.27 us
    ppermute x1, waiting for transfers between devices, per_device(): edge_far_halo = lax.ppermute(edge_far, 'lon', far_pairs)  1.03 us
  transfers between devices with their start and end apart: 6, of which 1 were waited for; matrix products, arithmetic and copies ran while one was open for 0% of the time, Pallas kernels for 32%

profile of v2, /device:TPU:0, one launch (start us, length us, event | category | flops | bytes accessed | tf_op | source)
XLA Modules:
  0.0 34.5 jit_solution(13811942048009601810)
XLA Ops:
  0.0 0.1 pad_add_fusion.par_ref.at_ref
  0.1 0.0 copy-start.3
  0.1 1.2 %copy-done.3 = bf16[1,2,42,12,512]{4,1,3,2,0:T(2,128)(2,1)S(1)} copy-done((bf16[1,2,42,12,512]{4,1,3,2,0:T(2,128)(2,1)S(1)}, bf16[1,2,42,12,512]{4,1,3,2,0:T(2,128)(2,1)}, u32[]{:S(2)}) %copy-start.3) | copy-done | bytes 1032216
  1.3 0.0 copy-start.5
  1.3 0.0 copy-start.6
  1.3 0.0 copy-start.9
  1.3 0.7 %pack.1 = (bf16[432,512]{1,0:T(8,128)(2,1)S(1)}, bf16[432,512]{1,0:T(8,128)(2,1)S(1)}, bf16[2,36,512]{2,1,0:T(8,128)(2,1)S(1)}, bf16[2,36,512]{2,1,0:T(8,128)(2,1)S(1)}) custom-call(s32[3]{0:T(128)S(1)} %pad_add_fusion.par_ref.at_ref, bf16[42,2,6,2,512]{4,3,2,1,0:T(2,128)(2,1)S(1)} %bitcast.16), custom_call_target="tpu_custom_call" | custom-call | flops 1000000000 | bytes 3000000 | tf_op jit(solution)/shard_map/pack/pallas_call | solution.py:61
  2.0 3.1 %collective-permute-start = (bf16[2,36,512]{2,1,0:T(8,128)(2,1)S(1)}, bf16[2,36,512]{2,1,0:T(8,128)(2,1)S(1)}, u32[]{:S(2)}, u32[]{:S(2)}) collective-permute-start(bf16[2,36,512]{2,1,0:T(8,128)(2,1)S(1)} %get-tuple-element.22.bot_ref), channel_id=1, source_target_pairs={{0,1},{1,2},{2,3},{3,0},{4,5},{5,6},{6,7},{7,4},{8,9},{9,10},{10,1... | collective-permute-start | bytes 221192 | tf_op jit(solution)/shard_map/ppermute | solution.py:439
  5.1 2.1 %collective-permute-start.1 = (bf16[2,36,512]{2,1,0:T(8,128)(2,1)S(1)}, bf16[2,36,512]{2,1,0:T(8,128)(2,1)S(1)}, u32[]{:S(2)}, u32[]{:S(2)}) collective-permute-start(bf16[2,36,512]{2,1,0:T(8,128)(2,1)S(1)} %get-tuple-element.23.top_ref), channel_id=1, source_target_pairs={{0,3},{1,0},{2,1},{3,2},{4,7},{5,4},{6,5},{7,6},{8,11},{9,8},{10,9... | collective-permute-start | bytes 221192 | tf_op jit(solution)/shard_map/ppermute | solution.py:440
  7.2 0.0 collective-permute-start.2
  7.2 2.7 %collective-permute-start.3 = (bf16[432,512]{1,0:T(8,128)(2,1)S(1)}, bf16[432,512]{1,0:T(8,128)(2,1)S(1)}, u32[]{:S(2)}, u32[]{:S(2)}) collective-permute-start(bf16[432,512]{1,0:T(8,128)(2,1)S(1)} %get-tuple-element.31.far), channel_id=1, source_target_pairs={{0,28},{4,8},{8,4},{12,16},{16,12},{20,24},{24,20},{28,0},{1,29},{... | collective-permute-start | bytes 1327112 | tf_op jit(solution)/shard_map/ppermute | solution.py:437
  9.9 0.0 copy-done.5
  9.9 0.0 copy-done.6
  9.9 0.0 copy-done.9
  9.9 0.0 copy-start
  9.9 0.0 copy-start.1
  9.9 0.0 copy-start.2
  9.9 0.0 copy-start.4
  9.9 0.0 copy-start.7
  9.9 0.0 copy-start.8
  9.9 4.2 %prep.1 = (f32[16,72,144]{2,1,0:T(8,128)S(1)}, f32[16,72,144]{2,1,0:T(8,128)S(1)}, f32[6,72,144]{2,1,0:T(8,128)S(1)}, f32[6,72,144]{2,1,0:T(8,128)S(1)}, f32[4,72,144]{2,1,0:T(8,128)S(1)}) custom-call(s32[3]{0:T(128)S(1)} %pad_add_fusion.par_ref.at_ref, s32[168,96]{1,0:T(8,128)S(1)} %copy-done.5, f32[16,759]{1,0:T(8,128)S(1)} %bitcast.17, ...), custom_call_target="tpu_custom_call" | custom-call | flops 5000000000 | bytes 15000000 | tf_op jit(solution)/shard_map/prep/pallas_call | solution.py:201
  14.1 0.0 collective-permute-done.above_ref
  14.1 0.0 collective-permute-done.1.below_ref
  14.2 0.1 edge_pack.1
  14.2 0.1 collective-permute-start.4
  14.3 0.6 %collective-permute-start.5 = (bf16[144,512]{1,0:T(8,128)(2,1)S(1)}, bf16[144,512]{1,0:T(8,128)(2,1)S(1)}, u32[]{:S(2)}, u32[]{:S(2)}) collective-permute-start(bf16[144,512]{1,0:T(8,128)(2,1)S(1)} %get-tuple-element.33.e_far), channel_id=1, source_target_pairs={{0,28},{4,8},{8,4},{12,16},{16,12},{20,24},{24,20},{28,0},{1,29},{... | collective-permute-start | bytes 442376 | tf_op jit(solution)/shard_map/ppermute | solution.py:445
  14.9 0.0 collective-permute-done.2.halo
  14.9 0.0 copy-done
  14.9 0.0 copy-done.1
  14.9 0.0 copy-done.2
  14.9 0.0 copy-done.4
  14.9 0.0 copy-done.7
  15.0 0.0 copy-done.8
  15.0 6.9 %near.1.near_res = bf16[36,6,2,512]{3,2,1,0:T(2,128)(2,1)S(1)} custom-call(bf16[432,512]{1,0:T(8,128)(2,1)S(1)} %get-tuple-element.28.own, bf16[432,512]{1,0:T(8,128)(2,1)S(1)} %collective-permute-done.2.halo, f32[16,72,144]{2,1,0:T(8,128)S(1)} %get-tuple-element.29.bias.refs_0_, f32[6,72,144]{2,1,0:T(8,128)S(1)} %get-tuple-element.30.mask, ...), custom_call_target="tpu_custom_call" | custom-call | flops 8000000000 | bytes 24000000 | tf_op jit(solution)/shard_map/near/pallas_call | solution.py:387
  21.9 0.0 collective-permute-done.4.e_near_halo
  21.9 1.0 %collective-permute-done.5.e_far_halo = bf16[144,512]{1,0:T(8,128)(2,1)S(1)} collective-permute-done((bf16[144,512]{1,0:T(8,128)(2,1)S(1)}, bf16[144,512]{1,0:T(8,128)(2,1)S(1)}, u32[]{:S(2)}, u32[]{:S(2)}) %collective-permute-start.5) | collective-permute-done | bytes 147488 | tf_op jit(solution)/shard_map/ppermute | solution.py:445
  23.0 0.0 collective-permute-done.3.far_halo
  23.0 11.4 %last.1 = bf16[42,2,6,2,512]{4,3,2,1,0:T(2,128)(2,1)} custom-call(s32[3]{0:T(128)S(1)} %pad_add_fusion.par_ref.at_ref, bf16[36,6,2,512]{3,2,1,0:T(2,128)(2,1)S(1)} %near.1.near_res, bf16[432,512]{1,0:T(8,128)(2,1)S(1)} %get-tuple-element.31.far, bf16[432,512]{1,0:T(8,128)(2,1)S(1)} %collective-permute-done.3.far_halo, ...), custom_call_target="tpu_custom_call" | custom-call | flops 12000000000 | bytes 36000000 | tf_op jit(solution)/shard_map/last/pallas_call | solution.py:403
Async XLA Ops:
  0.1 1.2 %copy-start.3 = (bf16[1,2,42,12,512]{4,1,3,2,0:T(2,128)(2,1)S(1)}, bf16[1,2,42,12,512]{4,1,3,2,0:T(2,128)(2,1)}, u32[]{:S(2)}) copy-start(bf16[1,2,42,12,512]{4,1,3,2,0:T(2,128)(2,1)} %param.10) | copy-start | bytes 3096580
  1.3 8.6 %copy-start.5 = (s32[168,96]{1,0:T(8,128)S(1)}, s32[168,96]{1,0:T(8,128)}, u32[]{:S(2)}) copy-start(s32[168,96]{1,0:T(8,128)} %gid_any.1) | copy-start | bytes 193540
  1.3 8.6 %copy-start.6 = (f32[759,16]{0,1:T(8,128)S(1)}, f32[759,16]{0,1:T(8,128)}, u32[]{:S(2)}) copy-start(f32[759,16]{0,1:T(8,128)} %param.12) | copy-start | bytes 145732
  1.3 8.6 %copy-start.9 = (bf16[768,768]{1,0:T(8,128)(2,1)S(1)}, bf16[768,768]{1,0:T(8,128)(2,1)}, u32[]{:S(2)}) copy-start(bf16[768,768]{1,0:T(8,128)(2,1)} %constant.16.clone.spread_any) | copy-start | bytes 3538948
  2.0 12.1 %collective-permute-start = (bf16[2,36,512]{2,1,0:T(8,128)(2,1)S(1)}, bf16[2,36,512]{2,1,0:T(8,128)(2,1)S(1)}, u32[]{:S(2)}, u32[]{:S(2)}) collective-permute-start(bf16[2,36,512]{2,1,0:T(8,128)(2,1)S(1)} %get-tuple-element.22.bot_ref), channel_id=1, source_target_pairs={{0,1},{1,2},{2,3},{3,0},{4,5},{5,6},{6,7},{7,4},{8,9},{9,10},{10,1... | collective-permute-start | bytes 221192 | tf_op jit(solution)/shard_map/ppermute | solution.py:439
  5.1 9.1 %collective-permute-start.1 = (bf16[2,36,512]{2,1,0:T(8,128)(2,1)S(1)}, bf16[2,36,512]{2,1,0:T(8,128)(2,1)S(1)}, u32[]{:S(2)}, u32[]{:S(2)}) collective-permute-start(bf16[2,36,512]{2,1,0:T(8,128)(2,1)S(1)} %get-tuple-element.23.top_ref), channel_id=1, source_target_pairs={{0,3},{1,0},{2,1},{3,2},{4,7},{5,4},{6,5},{7,6},{8,11},{9,8},{10,9... | collective-permute-start | bytes 221192 | tf_op jit(solution)/shard_map/ppermute | solution.py:440
  7.2 7.8 %collective-permute-start.2 = (bf16[432,512]{1,0:T(8,128)(2,1)S(1)}, bf16[432,512]{1,0:T(8,128)(2,1)S(1)}, u32[]{:S(2)}, u32[]{:S(2)}) collective-permute-start(bf16[432,512]{1,0:T(8,128)(2,1)S(1)} %get-tuple-element.28.own), channel_id=1, source_target_pairs={{0,4},{4,0},{8,12},{12,8},{16,20},{20,16},{24,28},{28,24},{1,5},{5... | collective-permute-start | bytes 1327112 | tf_op jit(solution)/shard_map/ppermute | solution.py:438
  7.2 15.8 %collective-permute-start.3 = (bf16[432,512]{1,0:T(8,128)(2,1)S(1)}, bf16[432,512]{1,0:T(8,128)(2,1)S(1)}, u32[]{:S(2)}, u32[]{:S(2)}) collective-permute-start(bf16[432,512]{1,0:T(8,128)(2,1)S(1)} %get-tuple-element.31.far), channel_id=1, source_target_pairs={{0,28},{4,8},{8,4},{12,16},{16,12},{20,24},{24,20},{28,0},{1,29},{... | collective-permute-start | bytes 1327112 | tf_op jit(solution)/shard_map/ppermute | solution.py:437
  9.9 5.0 %copy-start = (bf16[512,2048]{1,0:T(8,128)(2,1)S(1)}, bf16[512,2048]{1,0:T(8,128)(2,1)}, u32[]{:S(2)}) copy-start(bf16[512,2048]{1,0:T(8,128)(2,1)} %refs_6_.1) | copy-start | bytes 6291460
  9.9 5.0 %copy-start.1 = (bf16[2048,512]{1,0:T(8,128)(2,1)S(1)}, bf16[2048,512]{1,0:T(8,128)(2,1)}, u32[]{:S(2)}) copy-start(bf16[2048,512]{1,0:T(8,128)(2,1)} %refs_7_.1) | copy-start | bytes 6291460
  9.9 5.0 %copy-start.2 = (bf16[512,1536]{1,0:T(8,128)(2,1)S(1)}, bf16[512,1536]{1,0:T(8,128)(2,1)}, u32[]{:S(2)}) copy-start(bf16[512,1536]{1,0:T(8,128)(2,1)} %refs_4_.1) | copy-start | bytes 4718596
  9.9 5.0 %copy-start.4 = (bf16[512,512]{1,0:T(8,128)(2,1)S(1)}, bf16[512,512]{1,0:T(8,128)(2,1)}, u32[]{:S(2)}) copy-start(bf16[512,512]{1,0:T(8,128)(2,1)} %refs_5_.1) | copy-start | bytes 1572868
  9.9 5.0 %copy-start.7 = (f32[512]{0:T(512)S(1)}, f32[512]{0:T(512)}, u32[]{:S(2)}) copy-start(f32[512]{0:T(512)} %param.15) | copy-start | bytes 6148
  9.9 5.0 %copy-start.8 = (f32[512]{0:T(512)S(1)}, f32[512]{0:T(512)}, u32[]{:S(2)}) copy-start(f32[512]{0:T(512)} %param.18) | copy-start | bytes 6148
  14.2 7.7 %collective-permute-start.4 = (bf16[144,512]{1,0:T(8,128)(2,1)S(1)}, bf16[144,512]{1,0:T(8,128)(2,1)S(1)}, u32[]{:S(2)}, u32[]{:S(2)}) collective-permute-start(bf16[144,512]{1,0:T(8,128)(2,1)S(1)} %get-tuple-element.32.e_near), channel_id=1, source_target_pairs={{0,4},{4,0},{8,12},{12,8},{16,20},{20,16},{24,28},{28,24},{1,5},{5... | collective-permute-start | bytes 442376 | tf_op jit(solution)/shard_map/ppermute | solution.py:444
  14.3 8.7 %collective-permute-start.5 = (bf16[144,512]{1,0:T(8,128)(2,1)S(1)}, bf16[144,512]{1,0:T(8,128)(2,1)S(1)}, u32[]{:S(2)}, u32[]{:S(2)}) collective-permute-start(bf16[144,512]{1,0:T(8,128)(2,1)S(1)} %get-tuple-element.33.e_far), channel_id=1, source_target_pairs={{0,28},{4,8},{8,4},{12,16},{16,12},{20,24},{24,20},{28,0},{1,29},{... | collective-permute-start | bytes 442376 | tf_op jit(solution)/shard_map/ppermute | solution.py:445

commit v3 on v2

--- a/solution.py
+++ b/solution.py
@@ -2,7 +2,6 @@
 
 import jax
 import jax.numpy as jnp
-import numpy as np
 from jax import lax
 from jax.experimental import pallas as pl
 from jax.experimental.pallas import tpu as pltpu
@@ -22,6 +21,9 @@
 KEYS = 2 * HALF
 SPREAD = 256
 GROUP = 4
+FF_CHUNK = 1024
+PREP_US = 2
+NEAR_US = 1
 VMEM_LIMIT = 24 * 1024 * 1024
 PACK_LIMIT = 20 * 1024 * 1024
 
@@ -35,10 +37,6 @@
 
 def cost(micros):
     return pl.CostEstimate(flops=int(micros * 1e9), bytes_accessed=int(micros * 3e6), transcendentals=0)
-
-
-def anywhere(count):
-    return [pl.BlockSpec(memory_space=pl.ANY)] * count
 
 
 def vmem(count):
@@ -94,45 +92,14 @@
     )(above, top, bot, below)
 
 
-def spread_matrix(count):
-    nw, nh = 2 * WIN_LON - 1, 2 * WIN_LAT - 1
-    out = np.zeros((count, 3, SPREAD), np.float32)
-    for kind, centre in enumerate((WIN_LON - 1, SHIFT_LON - 1, WIN_LON + SHIFT_LON - 1)):
-        for j in range(nh):
-            for w in range(SHIFT_LON):
-                for z in range(WIN_LEV):
-                    at = (WIN_LEV - 1 - z) * nh * nw + (nh - 1 - j) * nw + centre - w
-                    out[at, kind, j * ROW + w * WIN_LEV + z] = 1
-    return out.reshape(count, 3 * SPREAD)
-
-
 def prep_kernel(
-    at_ref,
-    gid_any,
-    table_any,
-    spread_any,
-    bias_near,
-    bias_far,
-    mask_near,
-    mask_far,
-    mask_edge,
-    wide,
-    kinds,
-    gid_ref,
-    table_ref,
-    spread_ref,
-    sems,
+    at_ref, gid_ref, table_ref, bias_near, bias_far, mask_near, mask_far, mask_edge, wide, kinds
 ):
-    pairs = ((table_any, table_ref), (gid_any, gid_ref), (spread_any, spread_ref))
-    copies = [pltpu.make_async_copy(src, dst, sems.at[i]) for i, (src, dst) in enumerate(pairs)]
-    for copy in copies:
-        copy.start()
     heads, offsets = table_ref.shape
     nw, nh = 2 * WIN_LON - 1, 2 * WIN_LAT - 1
     par, lat_at, lon_at = at_ref[0], at_ref[1], at_ref[2]
     count = wide.shape[1]
     wide[...] = jnp.zeros_like(wide)
-    copies[0].wait()
     wide[:, :offsets] = table_ref[...] * LOG2E
     x = jnp.broadcast_to(wide[...][:, None, :], (heads, 16, count)).reshape(heads * 16, count)
     place = lax.broadcasted_iota(jnp.int32, x.shape, 0) % 16
@@ -140,9 +107,13 @@
         x = jnp.where(bit == 1, pltpu.roll(x, count - amount, 1), x)
     high = x.astype(BF16)
     low = (x - high.astype(F32)).astype(BF16)
-    copies[2].wait()
-    for kind in range(3):
-        m = spread_ref[:, kind * SPREAD : (kind + 1) * SPREAD]
+    lane = lax.broadcasted_iota(jnp.int32, (1, SPREAD), 1)
+    j, w, z = lane // ROW, lane % ROW // WIN_LEV, lane % WIN_LEV
+    source = (WIN_LEV - 1 - z) * nh * nw + (nh - 1 - j) * nw - w
+    source = jnp.where(j < nh, source, -count)
+    offset = lax.broadcasted_iota(jnp.int32, (count, SPREAD), 0)
+    for kind, centre in enumerate((WIN_LON - 1, SHIFT_LON - 1, WIN_LON + SHIFT_LON - 1)):
+        m = jnp.where(offset == source + centre, 1.0, 0.0).astype(BF16)
         y = jnp.dot(high, m, preferred_element_type=F32) + jnp.dot(low, m, preferred_element_type=F32)
         kinds[kind] = y.reshape(heads, 16, SPREAD)
     for side, out in enumerate((bias_near, bias_far)):
@@ -151,7 +122,6 @@
             start = (WIN_LAT - 1 - h) * ROW
             out[:, h * ROW : (h + 1) * ROW, :HALF] = kinds[0, :, :ROW, start : start + HALF]
             out[:, h * ROW : (h + 1) * ROW, HALF:KEYS] = halo[:, :ROW, start : start + HALF]
-    copies[1].wait()
     total, around = gid_ref.shape
     wins = mask_near.shape[0] + 2
     lat_rows = (wins - 1) * WIN_LAT
@@ -197,10 +167,9 @@
 def prep(at, group_ids, table, wins):
     heads, offsets = table.shape
     count = -(-offsets // 256) * 256
-    spread = jnp.asarray(spread_matrix(count), BF16)
     return pl.pallas_call(
         prep_kernel,
-        in_specs=[pl.BlockSpec(memory_space=pltpu.SMEM)] + anywhere(3),
+        in_specs=[pl.BlockSpec(memory_space=pltpu.SMEM)] + vmem(2),
         out_specs=vmem(5),
         out_shape=[jax.ShapeDtypeStruct((heads, HALF, KEYS), F32)] * 2
         + [jax.ShapeDtypeStruct((wins - 2, HALF, KEYS), F32)] * 2
@@ -208,15 +177,11 @@
         scratch_shapes=[
             pltpu.VMEM((heads, count), F32),
             pltpu.VMEM((3, heads, 16, SPREAD), F32),
-            pltpu.VMEM(group_ids.shape, jnp.int32),
-            pltpu.VMEM(table.shape, F32),
-            pltpu.VMEM(spread.shape, BF16),
-            pltpu.SemaphoreType.DMA((3,)),
         ],
         compiler_params=params(),
-        cost_estimate=cost(5),
+        cost_estimate=cost(PREP_US),
         name="prep",
-    )(at, group_ids, table, spread)
+    )(at, group_ids, table)
 
 
 def norm_rows(value, gain):
@@ -237,6 +202,7 @@
     sc = sc + extra.reshape(GROUP * per, KEYS) + mask
     top = jnp.max(sc, -1, keepdims=True)
     p = jnp.exp2(sc - top).astype(BF16)
+    v = jnp.concatenate([v, jnp.ones(v.shape, BF16)], 1)
     o = jnp.dot(p, v, preferred_element_type=F32)
     num, den = o[:per, :lanes], o[:per, lanes:]
     for j in range(1, GROUP):
@@ -257,9 +223,6 @@
     scale = LOG2E / hd**0.5
     step = 2 * lanes
     wi = 0
-    for g in range(groups):
-        ones = jnp.ones((v_scr.shape[0], KEYS, lanes), BF16)
-        v_scr[:, :, (2 * g + 1) * lanes : (2 * g + 2) * lanes] = ones
     base = 0
     for own, halo, bias, mask_ref, mask_at, q_lo, q_rows in blocks:
         wins = own.shape[0] // HALF
@@ -278,8 +241,7 @@
                     if part == d:
                         k_scr[wi + i, :, c : c + step] = both
                     else:
-                        v_scr[wi + i, :, 2 * c : 2 * c + lanes] = both[:, :lanes]
-                        v_scr[wi + i, :, 2 * c + step : 2 * c + step + lanes] = both[:, lanes:]
+                        v_scr[wi + i, :, c : c + step] = both
         lane_head = lax.broadcasted_iota(jnp.int32, (per, lanes), 1) // hd
         for i in range(wins):
             first = q_lo + i * per - i * HALF
@@ -289,7 +251,7 @@
                 o_scr[at : at + per, g * lanes : (g + 1) * lanes] = attend(
                     q_scr[at : at + per, g * lanes : (g + 1) * lanes],
                     k_scr[wi + i, :, g * lanes : (g + 1) * lanes],
-                    v_scr[wi + i, :, 2 * g * lanes : (2 * g + 2) * lanes],
+                    v_scr[wi + i, :, g * lanes : (g + 1) * lanes],
                     bias[g * GROUP : (g + 1) * GROUP, first : first + per, :],
                     mask,
                     lane_head,
@@ -306,7 +268,7 @@
         ).astype(BF16)
         base += q_rows
     ff = w_in.shape[1]
-    chunk = 256
+    chunk = FF_CHUNK
     for c in range(0, ff, chunk):
         up = jnp.dot(mid_scr[...], w_in[:, c : c + chunk], preferred_element_type=F32)
         hid = gelu(up).astype(BF16)
@@ -322,7 +284,7 @@
     weights, out, scratch = refs[:6], refs[6], refs[7:]
     rows, d = own.shape
     res = layer_body([(own, halo, bias, mask, 0, 0, rows)], weights, scratch)
-    out[...] = res.reshape(out.shape).astype(BF16)
+    out[...] = res.astype(BF16).reshape(out.shape)
 
 
 def last_kernel(
@@ -348,7 +310,7 @@
         weights,
         scratch,
     )
-    far_buf[...] = res[:rows].reshape(far_buf.shape).astype(BF16)
+    far_buf[...] = res[:rows].astype(BF16).reshape(far_buf.shape)
     copies = [pltpu.make_async_copy(far_buf, out.at[main, halves[1]], sems.at[4])]
     copies[0].start()
     shape = edge_buf.shape[2:]
@@ -374,7 +336,7 @@
     return [
         pltpu.VMEM((total, d), F32),
         pltpu.VMEM((windows, KEYS, d), BF16),
-        pltpu.VMEM((windows, KEYS, 2 * d), BF16),
+        pltpu.VMEM((windows, KEYS, d), BF16),
         pltpu.VMEM((total, d), F32),
         pltpu.VMEM((total, d), BF16),
         pltpu.VMEM((total, d), F32),
@@ -391,7 +353,7 @@
         out_shape=jax.ShapeDtypeStruct(shape, BF16),
         scratch_shapes=layer_scratch(rows, rows // HALF, weights),
         compiler_params=params(),
-        cost_estimate=cost(8),
+        cost_estimate=cost(NEAR_US),
         name="near",
     )(own, halo, bias, mask, *weights)
 

time: 34.7 us -> 32 us (0.922)
  Pallas kernels: 23.2 us -> 21.6 us
  waiting for transfers between devices: 1.04 us -> 0.02 us
    ppermute x1, starting transfers between devices: 3.08 us -> 1.58 us  [per_device(): above = lax.ppermute(bot, 'lat', down_pairs)]
    ppermute x1, waiting for transfers between devices: 1.03 us -> 0.01 us  [per_device(): edge_far_halo = lax.ppermute(edge_far, 'lon', far_pairs)]
    ppermute x1, starting transfers between devices: 2.72 us -> 3.56 us  [per_device(): far_halo = lax.ppermute(far, 'lon', far_pairs)]
    pallas_call x1, Pallas kernels: 11.4 us -> 10.7 us  [last_layer(): pl.pallas_call(last_kernel, in_specs=[pl.BlockSpec(memory_space=pltpu.SME...]
    pallas_call x1, Pallas kernels: 6.94 us -> 6.39 us  [near_layer(): pl.pallas_call(near_kernel, in_specs=vmem(10), out_specs=vmem(1)[0], out_...]
    ppermute x1, starting transfers between devices: 0.01 us -> 0.52 us  [per_device(): near_halo = lax.ppermute(near, 'lon', near_pairs)]
    pallas_call x1, Pallas kernels: 4.17 us -> 3.75 us  [prep(): pl.pallas_call(prep_kernel, in_specs=[pl.BlockSpec(memory_space=pltpu.SME...]
    unnamed x20 -> x18, local copies, waits for them, and re-layouts: 1.27 us -> 1.26 us
  transfers between devices with their start and end apart: 6 -> 6, of which waited for: 1 -> 0; matrix products, arithmetic and copies ran while one was open for 0% -> 0% of each run, Pallas kernels for 32% -> 32%
where the time goes in v3:
time: 32 us; the launch traced here: 31.8 us
  Pallas kernels  21.6 us (68%)
  starting transfers between devices  8.61 us (27%)
  local copies, waits for them, and re-layouts  1.26 us (4%)
    pallas_call x1, Pallas kernels, last_layer(): pl.pallas_call(last_kernel, in_specs=[pl.BlockSpec(memory_space=pltpu.SME...  10.7 us
    pallas_call x1, Pallas kernels, near_layer(): pl.pallas_call(near_kernel, in_specs=vmem(10), out_specs=vmem(1)[0], out_...  6.39 us
    pallas_call x1, Pallas kernels, prep(): pl.pallas_call(prep_kernel, in_specs=[pl.BlockSpec(memory_space=pltpu.SME...  3.75 us
    ppermute x1, starting transfers between devices, per_device(): far_halo = lax.ppermute(far, 'lon', far_pairs)  3.56 us
    ppermute x1, starting transfers between devices, per_device(): below = lax.ppermute(top, 'lat', up_pairs)  2.25 us
    ppermute x1, starting transfers between devices, per_device(): above = lax.ppermute(bot, 'lat', down_pairs)  1.58 us
    unnamed x18, local copies, waits for them, and re-layouts  1.26 us
    pallas_call x1, Pallas kernels, pack(): pl.pallas_call(pack_kernel, in_specs=[pl.BlockSpec(memory_space=pltpu.SME...  0.67 us
  transfers between devices with their start and end apart: 6, of which 0 were waited for; matrix products, arithmetic and copies ran while one was open for 0% of the time, Pallas kernels for 32%

profile of v3, /device:TPU:0, one launch (start us, length us, event | category | flops | bytes accessed | tf_op | source)
XLA Modules:
  0.0 31.8 jit_solution(10539592939101871327)
XLA Ops:
  0.0 0.1 pad_add_fusion.par_ref.at_ref
  0.1 0.0 copy-start.6
  0.1 1.2 %copy-done.6 = bf16[1,2,42,12,512]{4,1,3,2,0:T(2,128)(2,1)S(1)} copy-done((bf16[1,2,42,12,512]{4,1,3,2,0:T(2,128)(2,1)S(1)}, bf16[1,2,42,12,512]{4,1,3,2,0:T(2,128)(2,1)}, u32[]{:S(2)}) %copy-start.6) | copy-done | bytes 1032216
  1.3 0.0 copy-start.7
  1.3 0.0 copy-start.8
  1.3 0.7 %pack.1 = (bf16[432,512]{1,0:T(8,128)(2,1)S(1)}, bf16[432,512]{1,0:T(8,128)(2,1)S(1)}, bf16[2,36,512]{2,1,0:T(8,128)(2,1)S(1)}, bf16[2,36,512]{2,1,0:T(8,128)(2,1)S(1)}) custom-call(s32[3]{0:T(128)S(1)} %pad_add_fusion.par_ref.at_ref, bf16[42,2,6,2,512]{4,3,2,1,0:T(2,128)(2,1)S(1)} %bitcast.20), custom_call_target="tpu_custom_call" | custom-call | flops 1000000000 | bytes 3000000 | tf_op jit(solution)/shard_map/pack/pallas_call | solution.py:59
  2.0 0.5 %collective-permute-start.2 = (bf16[432,512]{1,0:T(8,128)(2,1)S(1)}, bf16[432,512]{1,0:T(8,128)(2,1)S(1)}, u32[]{:S(2)}, u32[]{:S(2)}) collective-permute-start(bf16[432,512]{1,0:T(8,128)(2,1)S(1)} %get-tuple-element.28.own), channel_id=1, source_target_pairs={{0,4},{4,0},{8,12},{12,8},{16,20},{20,16},{24,28},{28,24},{1,5},{5... | collective-permute-start | bytes 1327112 | tf_op jit(solution)/shard_map/ppermute | solution.py:400
  2.5 3.6 %collective-permute-start.3 = (bf16[432,512]{1,0:T(8,128)(2,1)S(1)}, bf16[432,512]{1,0:T(8,128)(2,1)S(1)}, u32[]{:S(2)}, u32[]{:S(2)}) collective-permute-start(bf16[432,512]{1,0:T(8,128)(2,1)S(1)} %get-tuple-element.31.far), channel_id=1, source_target_pairs={{0,28},{4,8},{8,4},{12,16},{16,12},{20,24},{24,20},{28,0},{1,29},{... | collective-permute-start | bytes 1327112 | tf_op jit(solution)/shard_map/ppermute | solution.py:399
  6.1 1.6 %collective-permute-start = (bf16[2,36,512]{2,1,0:T(8,128)(2,1)S(1)}, bf16[2,36,512]{2,1,0:T(8,128)(2,1)S(1)}, u32[]{:S(2)}, u32[]{:S(2)}) collective-permute-start(bf16[2,36,512]{2,1,0:T(8,128)(2,1)S(1)} %get-tuple-element.22.bot_ref), channel_id=1, source_target_pairs={{0,1},{1,2},{2,3},{3,0},{4,5},{5,6},{6,7},{7,4},{8,9},{9,10},{10,1... | collective-permute-start | bytes 221192 | tf_op jit(solution)/shard_map/ppermute | solution.py:401
  7.6 2.2 %collective-permute-start.1 = (bf16[2,36,512]{2,1,0:T(8,128)(2,1)S(1)}, bf16[2,36,512]{2,1,0:T(8,128)(2,1)S(1)}, u32[]{:S(2)}, u32[]{:S(2)}) collective-permute-start(bf16[2,36,512]{2,1,0:T(8,128)(2,1)S(1)} %get-tuple-element.23.top_ref), channel_id=1, source_target_pairs={{0,3},{1,0},{2,1},{3,2},{4,7},{5,4},{6,5},{7,6},{8,11},{9,8},{10,9... | collective-permute-start | bytes 221192 | tf_op jit(solution)/shard_map/ppermute | solution.py:402
  9.9 0.0 copy-done.7
  9.9 0.0 copy-done.8
  9.9 0.0 copy-start
  9.9 0.0 copy-start.1
  9.9 0.0 copy-start.2
  9.9 0.0 copy-start.3
  9.9 0.0 copy-start.4
  9.9 0.0 copy-start.5
  9.9 3.8 %prep.1 = (f32[16,72,144]{2,1,0:T(8,128)S(1)}, f32[16,72,144]{2,1,0:T(8,128)S(1)}, f32[6,72,144]{2,1,0:T(8,128)S(1)}, f32[6,72,144]{2,1,0:T(8,128)S(1)}, f32[4,72,144]{2,1,0:T(8,128)S(1)}) custom-call(s32[3]{0:T(128)S(1)} %pad_add_fusion.par_ref.at_ref, s32[168,96]{1,0:T(8,128)S(1)} %copy-done.7, f32[16,759]{1,0:T(8,128)S(1)} %bitcast.21), custom_call_target="tpu_custom_call" | custom-call | flops 2000000000 | bytes 6000000 | tf_op jit(solution)/shard_map/prep/pallas_call | solution.py:170
  13.7 0.0 collective-permute-done.above_ref
  13.7 0.0 collective-permute-done.1.below_ref
  13.8 0.1 collective-permute-start.4
  13.9 0.6 %collective-permute-start.5 = (bf16[144,512]{1,0:T(8,128)(2,1)S(1)}, bf16[144,512]{1,0:T(8,128)(2,1)S(1)}, u32[]{:S(2)}, u32[]{:S(2)}) collective-permute-start(bf16[144,512]{1,0:T(8,128)(2,1)S(1)} %get-tuple-element.33.e_far), channel_id=1, source_target_pairs={{0,28},{4,8},{8,4},{12,16},{16,12},{20,24},{24,20},{28,0},{1,29},{... | collective-permute-start | bytes 442376 | tf_op jit(solution)/shard_map/ppermute | solution.py:407
  14.5 0.0 collective-permute-done.2.halo
  14.5 0.0 copy-done
  14.5 0.0 copy-done.1
  14.5 0.0 copy-done.2
  14.5 0.0 copy-done.3
  14.5 0.0 copy-done.4
  14.5 0.0 copy-done.5
  14.5 6.4 %near.1.near_res = bf16[36,6,2,512]{3,2,1,0:T(2,128)(2,1)S(1)} custom-call(bf16[432,512]{1,0:T(8,128)(2,1)S(1)} %get-tuple-element.28.own, bf16[432,512]{1,0:T(8,128)(2,1)S(1)} %collective-permute-done.2.halo, f32[16,72,144]{2,1,0:T(8,128)S(1)} %get-tuple-element.29.bias.refs_0_, f32[6,72,144]{2,1,0:T(8,128)S(1)} %get-tuple-element.30.mask, ...), custom_call_target="tpu_custom_call" | custom-call | flops 1000000000 | bytes 3000000 | tf_op jit(solution)/shard_map/near/pallas_call | solution.py:349
  20.9 0.0 collective-permute-done.4.e_near_halo
  21.0 0.0 collective-permute-done.5.e_far_halo
  21.0 0.0 collective-permute-done.3.far_halo
  21.0 10.7 %last.1 = bf16[42,2,6,2,512]{4,3,2,1,0:T(2,128)(2,1)} custom-call(s32[3]{0:T(128)S(1)} %pad_add_fusion.par_ref.at_ref, bf16[36,6,2,512]{3,2,1,0:T(2,128)(2,1)S(1)} %near.1.near_res, bf16[432,512]{1,0:T(8,128)(2,1)S(1)} %get-tuple-element.31.far, bf16[432,512]{1,0:T(8,128)(2,1)S(1)} %collective-permute-done.3.far_halo, ...), custom_call_target="tpu_custom_call" | custom-call | flops 12000000000 | bytes 36000000 | tf_op jit(solution)/shard_map/last/pallas_call | solution.py:365
  (1 shorter events, 0.0 us)
Async XLA Ops:
  0.1 1.2 %copy-start.6 = (bf16[1,2,42,12,512]{4,1,3,2,0:T(2,128)(2,1)S(1)}, bf16[1,2,42,12,512]{4,1,3,2,0:T(2,128)(2,1)}, u32[]{:S(2)}) copy-start(bf16[1,2,42,12,512]{4,1,3,2,0:T(2,128)(2,1)} %param.9) | copy-start | bytes 3096580
  1.3 8.6 %copy-start.7 = (s32[168,96]{1,0:T(8,128)S(1)}, s32[168,96]{1,0:T(8,128)}, u32[]{:S(2)}) copy-start(s32[168,96]{1,0:T(8,128)} %gid_ref.1) | copy-start | bytes 193540
  1.3 8.6 %copy-start.8 = (f32[759,16]{0,1:T(8,128)S(1)}, f32[759,16]{0,1:T(8,128)}, u32[]{:S(2)}) copy-start(f32[759,16]{0,1:T(8,128)} %param.11) | copy-start | bytes 145732
  2.0 12.5 %collective-permute-start.2 = (bf16[432,512]{1,0:T(8,128)(2,1)S(1)}, bf16[432,512]{1,0:T(8,128)(2,1)S(1)}, u32[]{:S(2)}, u32[]{:S(2)}) collective-permute-start(bf16[432,512]{1,0:T(8,128)(2,1)S(1)} %get-tuple-element.28.own), channel_id=1, source_target_pairs={{0,4},{4,0},{8,12},{12,8},{16,20},{20,16},{24,28},{28,24},{1,5},{5... | collective-permute-start | bytes 1327112 | tf_op jit(solution)/shard_map/ppermute | solution.py:400
  2.5 18.5 %collective-permute-start.3 = (bf16[432,512]{1,0:T(8,128)(2,1)S(1)}, bf16[432,512]{1,0:T(8,128)(2,1)S(1)}, u32[]{:S(2)}, u32[]{:S(2)}) collective-permute-start(bf16[432,512]{1,0:T(8,128)(2,1)S(1)} %get-tuple-element.31.far), channel_id=1, source_target_pairs={{0,28},{4,8},{8,4},{12,16},{16,12},{20,24},{24,20},{28,0},{1,29},{... | collective-permute-start | bytes 1327112 | tf_op jit(solution)/shard_map/ppermute | solution.py:399
  6.1 7.7 %collective-permute-start = (bf16[2,36,512]{2,1,0:T(8,128)(2,1)S(1)}, bf16[2,36,512]{2,1,0:T(8,128)(2,1)S(1)}, u32[]{:S(2)}, u32[]{:S(2)}) collective-permute-start(bf16[2,36,512]{2,1,0:T(8,128)(2,1)S(1)} %get-tuple-element.22.bot_ref), channel_id=1, source_target_pairs={{0,1},{1,2},{2,3},{3,0},{4,5},{5,6},{6,7},{7,4},{8,9},{9,10},{10,1... | collective-permute-start | bytes 221192 | tf_op jit(solution)/shard_map/ppermute | solution.py:401
  7.6 6.1 %collective-permute-start.1 = (bf16[2,36,512]{2,1,0:T(8,128)(2,1)S(1)}, bf16[2,36,512]{2,1,0:T(8,128)(2,1)S(1)}, u32[]{:S(2)}, u32[]{:S(2)}) collective-permute-start(bf16[2,36,512]{2,1,0:T(8,128)(2,1)S(1)} %get-tuple-element.23.top_ref), channel_id=1, source_target_pairs={{0,3},{1,0},{2,1},{3,2},{4,7},{5,4},{6,5},{7,6},{8,11},{9,8},{10,9... | collective-permute-start | bytes 221192 | tf_op jit(solution)/shard_map/ppermute | solution.py:402
  9.9 4.6 %copy-start = (bf16[512,2048]{1,0:T(8,128)(2,1)S(1)}, bf16[512,2048]{1,0:T(8,128)(2,1)}, u32[]{:S(2)}) copy-start(bf16[512,2048]{1,0:T(8,128)(2,1)} %refs_6_.1) | copy-start | bytes 6291460
  9.9 4.6 %copy-start.1 = (bf16[2048,512]{1,0:T(8,128)(2,1)S(1)}, bf16[2048,512]{1,0:T(8,128)(2,1)}, u32[]{:S(2)}) copy-start(bf16[2048,512]{1,0:T(8,128)(2,1)} %refs_7_.1) | copy-start | bytes 6291460
  9.9 4.6 %copy-start.2 = (bf16[512,1536]{1,0:T(8,128)(2,1)S(1)}, bf16[512,1536]{1,0:T(8,128)(2,1)}, u32[]{:S(2)}) copy-start(bf16[512,1536]{1,0:T(8,128)(2,1)} %refs_4_.1) | copy-start | bytes 4718596
  9.9 4.6 %copy-start.3 = (bf16[512,512]{1,0:T(8,128)(2,1)S(1)}, bf16[512,512]{1,0:T(8,128)(2,1)}, u32[]{:S(2)}) copy-start(bf16[512,512]{1,0:T(8,128)(2,1)} %refs_5_.1) | copy-start | bytes 1572868
  9.9 4.6 %copy-start.4 = (f32[512]{0:T(512)S(1)}, f32[512]{0:T(512)}, u32[]{:S(2)}) copy-start(f32[512]{0:T(512)} %param.14) | copy-start | bytes 6148
  9.9 4.6 %copy-start.5 = (f32[512]{0:T(512)S(1)}, f32[512]{0:T(512)}, u32[]{:S(2)}) copy-start(f32[512]{0:T(512)} %param.17) | copy-start | bytes 6148
  13.8 7.2 %collective-permute-start.4 = (bf16[144,512]{1,0:T(8,128)(2,1)S(1)}, bf16[144,512]{1,0:T(8,128)(2,1)S(1)}, u32[]{:S(2)}, u32[]{:S(2)}) collective-permute-start(bf16[144,512]{1,0:T(8,128)(2,1)S(1)} %get-tuple-element.32.e_near), channel_id=1, source_target_pairs={{0,4},{4,0},{8,12},{12,8},{16,20},{20,16},{24,28},{28,24},{1,5},{5... | collective-permute-start | bytes 442376 | tf_op jit(solution)/shard_map/ppermute | solution.py:406
  13.9 7.1 %collective-permute-start.5 = (bf16[144,512]{1,0:T(8,128)(2,1)S(1)}, bf16[144,512]{1,0:T(8,128)(2,1)S(1)}, u32[]{:S(2)}, u32[]{:S(2)}) collective-permute-start(bf16[144,512]{1,0:T(8,128)(2,1)S(1)} %get-tuple-element.33.e_far), channel_id=1, source_target_pairs={{0,28},{4,8},{8,4},{12,16},{16,12},{20,24},{24,20},{28,0},{1,29},{... | collective-permute-start | bytes 442376 | tf_op jit(solution)/shard_map/ppermute | solution.py:407

commit v4 on v3

--- a/solution.py
+++ b/solution.py
@@ -101,27 +101,36 @@
     count = wide.shape[1]
     wide[...] = jnp.zeros_like(wide)
     wide[:, :offsets] = table_ref[...] * LOG2E
-    x = jnp.broadcast_to(wide[...][:, None, :], (heads, 16, count)).reshape(heads * 16, count)
-    place = lax.broadcasted_iota(jnp.int32, x.shape, 0) % 16
-    for amount, bit in ((nh * nw, place % 2), (1, place // 2 % 2), (2, place // 4 % 2), (4, place // 8)):
+    rows = (heads, 16, count)
+    first = jnp.broadcast_to(wide[...][:, None, :], rows).reshape(heads * 16, count)
+    later = pltpu.roll(wide[...], count - nh * nw, 1)
+    later = jnp.broadcast_to(later[:, None, :], rows).reshape(heads * 16, count)
+    place = lax.broadcasted_iota(jnp.int32, first.shape, 0) % 16
+    x = jnp.where(place % 2 == 1, later, first)
+    for amount, bit in ((1, place // 2 % 2), (2, place // 4 % 2), (4, place // 8)):
         x = jnp.where(bit == 1, pltpu.roll(x, count - amount, 1), x)
     high = x.astype(BF16)
     low = (x - high.astype(F32)).astype(BF16)
     lane = lax.broadcasted_iota(jnp.int32, (1, SPREAD), 1)
     j, w, z = lane // ROW, lane % ROW // WIN_LEV, lane % WIN_LEV
     source = (WIN_LEV - 1 - z) * nh * nw + (nh - 1 - j) * nw - w
+    ahead = source + WIN_LAT * nw
     source = jnp.where(j < nh, source, -count)
+    ahead = jnp.where((j >= WIN_LAT) & (j < nh + WIN_LAT), ahead, -count)
     offset = lax.broadcasted_iota(jnp.int32, (count, SPREAD), 0)
     for kind, centre in enumerate((WIN_LON - 1, SHIFT_LON - 1, WIN_LON + SHIFT_LON - 1)):
-        m = jnp.where(offset == source + centre, 1.0, 0.0).astype(BF16)
+        m = jnp.where(offset == (ahead if kind else source) + centre, 1.0, 0.0).astype(BF16)
         y = jnp.dot(high, m, preferred_element_type=F32) + jnp.dot(low, m, preferred_element_type=F32)
-        kinds[kind] = y.reshape(heads, 16, SPREAD)
+        kinds[kind] = y
     for side, out in enumerate((bias_near, bias_far)):
         halo = kinds[2 - par if side else 1 + par]
         for h in range(WIN_LAT):
             start = (WIN_LAT - 1 - h) * ROW
-            out[:, h * ROW : (h + 1) * ROW, :HALF] = kinds[0, :, :ROW, start : start + HALF]
-            out[:, h * ROW : (h + 1) * ROW, HALF:KEYS] = halo[:, :ROW, start : start + HALF]
+            both = jnp.where(lane < HALF + start, kinds[0], halo)
+            if start:
+                both = pltpu.roll(both, SPREAD - start, 1)
+            both = both.reshape(heads, 16, SPREAD)
+            out[:, h * ROW : (h + 1) * ROW, :] = both[:, :ROW, :KEYS]
     total, around = gid_ref.shape
     wins = mask_near.shape[0] + 2
     lat_rows = (wins - 1) * WIN_LAT
@@ -130,8 +139,16 @@
     rest = jnp.where(is_halo, lane - HALF, lane)
     h_of = rest // ROW
     w_of = rest % ROW // WIN_LEV
-    ids = gid_ref[...].astype(BF16)
-    row = lax.broadcasted_iota(jnp.int32, (total, KEYS), 0)
+    span = wins * WIN_LAT
+    place = lat_at * lat_rows - WIN_LAT + lax.broadcasted_iota(jnp.int32, (span, 1), 0)
+    place = jnp.where(place < 0, place + total, place)
+    pick = jnp.where(lax.broadcasted_iota(jnp.int32, (span, total), 1) == place, 1.0, 0.0)
+    ids = jnp.dot(pick.astype(BF16), gid_ref[...].astype(BF16), preferred_element_type=F32).astype(BF16)
+    region = jnp.where(place >= total - SHIFT_LAT, 1.0, 0.0)
+    row = lax.broadcasted_iota(jnp.int32, (span, KEYS), 0)
+    window = lax.broadcasted_iota(jnp.int32, (wins, span), 0)
+    inside = lax.broadcasted_iota(jnp.int32, (wins, span), 1) // WIN_LAT
+    gather = jnp.where(window == inside, 1.0, 0.0).astype(BF16)
     col = lax.broadcasted_iota(jnp.int32, (around, KEYS), 0)
     for side in range(2):
         right = par == side
@@ -142,14 +159,8 @@
         want = jnp.where(want < 0, want + around, want)
         pick = jnp.where(col == want, 1.0, 0.0).astype(BF16)
         label = 2.0 * jnp.dot(ids, pick, preferred_element_type=F32)
-        label = label + jnp.where(row >= total - SHIFT_LAT, 1.0, 0.0)
-        lines = []
-        for k in range(wins):
-            want = lat_at * lat_rows + (k - 1) * WIN_LAT + h_of
-            want = jnp.where(want < 0, want + total, want)
-            line = jnp.sum(jnp.where(row == want, label, 0.0), 0, keepdims=True)
-            lines.append(line)
-        lines = jnp.concatenate(lines, 0)
+        label = jnp.where(row % WIN_LAT == h_of, label + region, 0.0).astype(BF16)
+        lines = jnp.dot(gather, label, preferred_element_type=F32)
         cols = lines[:, :128].T
         for k in range(wins):
             same = cols[:HALF, k : k + 1] == lines[k : k + 1, :]
@@ -176,7 +187,7 @@
         + [jax.ShapeDtypeStruct((4, HALF, KEYS), F32)],
         scratch_shapes=[
             pltpu.VMEM((heads, count), F32),
-            pltpu.VMEM((3, heads, 16, SPREAD), F32),
+            pltpu.VMEM((3, heads * 16, SPREAD), F32),
         ],
         compiler_params=params(),
         cost_estimate=cost(PREP_US),
@@ -222,26 +233,28 @@
     groups = heads // GROUP
     scale = LOG2E / hd**0.5
     step = 2 * lanes
+    asking = jnp.concatenate([own[q_lo : q_lo + n, :] for own, _, _, _, _, q_lo, n in blocks], 0)
+    rows = jnp.concatenate([ref[...] for own, halo, *_ in blocks for ref in (own, halo)], 0)
+    for c in range(0, d, step):
+        q = jnp.dot(asking, w_qkv[:, c : c + step], preferred_element_type=F32)
+        q_scr[:, c : c + step] = q * scale
+        for part, scr in ((d, k_scr), (2 * d, v_scr)):
+            y = jnp.dot(rows, w_qkv[:, part + c : part + c + step], preferred_element_type=F32)
+            at = 0
+            wi = 0
+            for own, halo, *_ in blocks:
+                size = own.shape[0]
+                for i in range(size // HALF):
+                    a = y[at + i * HALF : at + (i + 1) * HALF]
+                    b = y[at + size + i * HALF : at + size + (i + 1) * HALF]
+                    scr[wi, :, c : c + step] = jnp.concatenate([a, b], 0).astype(BF16)
+                    wi += 1
+                at += 2 * size
+    base = 0
     wi = 0
-    base = 0
     for own, halo, bias, mask_ref, mask_at, q_lo, q_rows in blocks:
         wins = own.shape[0] // HALF
         per = q_rows // wins
-        for c in range(0, d, step):
-            q = jnp.dot(own[q_lo : q_lo + q_rows, :], w_qkv[:, c : c + step], preferred_element_type=F32)
-            q_scr[base : base + q_rows, c : c + step] = q * scale
-            for part in (d, 2 * d):
-                w = w_qkv[:, part + c : part + c + step]
-                a = jnp.dot(own[...], w, preferred_element_type=F32)
-                b = jnp.dot(halo[...], w, preferred_element_type=F32)
-                for i in range(wins):
-                    both = jnp.concatenate(
-                        [a[i * HALF : (i + 1) * HALF], b[i * HALF : (i + 1) * HALF]], 0
-                    ).astype(BF16)
-                    if part == d:
-                        k_scr[wi + i, :, c : c + step] = both
-                    else:
-                        v_scr[wi + i, :, c : c + step] = both
         lane_head = lax.broadcasted_iota(jnp.int32, (per, lanes), 1) // hd
         for i in range(wins):
             first = q_lo + i * per - i * HALF

time: 32 us -> 31.2 us (0.975)
  Pallas kernels: 21.6 us -> 20.6 us
    pallas_call x1, Pallas kernels: 10.7 us -> 10.2 us  [last_layer(): pl.pallas_call(last_kernel, in_specs=[pl.BlockSpec(memory_space=pltpu.SME...]
    pallas_call x1, Pallas kernels: 3.75 us -> 3.35 us  [prep(): pl.pallas_call(prep_kernel, in_specs=[pl.BlockSpec(memory_space=pltpu.SME...]
  transfers between devices with their start and end apart: 6 -> 6, of which waited for: 0 -> 0; matrix products, arithmetic and copies ran while one was open for 0% -> 0% of each run, Pallas kernels for 32% -> 31%
where the time goes in v4:
time: 31.2 us; the launch traced here: 31 us
  Pallas kernels  20.6 us (66%)
  starting transfers between devices  8.76 us (28%)
  local copies, waits for them, and re-layouts  1.26 us (4%)
    pallas_call x1, Pallas kernels, last_layer(): pl.pallas_call(last_kernel, in_specs=[pl.BlockSpec(memory_space=pltpu.SME...  10.2 us
    pallas_call x1, Pallas kernels, near_layer(): pl.pallas_call(near_kernel, in_specs=vmem(10), out_specs=vmem(1)[0], out_...  6.36 us
    ppermute x1, starting transfers between devices, per_device(): far_halo = lax.ppermute(far, 'lon', far_pairs)  3.56 us
    pallas_call x1, Pallas kernels, prep(): pl.pallas_call(prep_kernel, in_specs=[pl.BlockSpec(memory_space=pltpu.SME...  3.35 us
    ppermute x1, starting transfers between devices, per_device(): below = lax.ppermute(top, 'lat', up_pairs)  2.25 us
    ppermute x1, starting transfers between devices, per_device(): above = lax.ppermute(bot, 'lat', down_pairs)  1.58 us
    unnamed x18, local copies, waits for them, and re-layouts  1.26 us
    ppermute x1, starting transfers between devices, per_device(): edge_far_halo = lax.ppermute(edge_far, 'lon', far_pairs)  0.8 us
  transfers between devices with their start and end apart: 6, of which 0 were waited for; matrix products, arithmetic and copies ran while one was open for 0% of the time, Pallas kernels for 31%

profile of v4, /device:TPU:0, one launch (start us, length us, event | category | flops | bytes accessed | tf_op | source)
XLA Modules:
  0.0 31.0 jit_solution(17247835110082694475)
XLA Ops:
  0.0 0.1 pad_add_fusion.par_ref.at_ref
  0.1 0.0 copy-start.6
  0.1 1.2 %copy-done.6 = bf16[1,2,42,12,512]{4,1,3,2,0:T(2,128)(2,1)S(1)} copy-done((bf16[1,2,42,12,512]{4,1,3,2,0:T(2,128)(2,1)S(1)}, bf16[1,2,42,12,512]{4,1,3,2,0:T(2,128)(2,1)}, u32[]{:S(2)}) %copy-start.6) | copy-done | bytes 1032216
  1.3 0.0 copy-start.7
  1.3 0.0 copy-start.8
  1.3 0.7 %pack.1 = (bf16[432,512]{1,0:T(8,128)(2,1)S(1)}, bf16[432,512]{1,0:T(8,128)(2,1)S(1)}, bf16[2,36,512]{2,1,0:T(8,128)(2,1)S(1)}, bf16[2,36,512]{2,1,0:T(8,128)(2,1)S(1)}) custom-call(s32[3]{0:T(128)S(1)} %pad_add_fusion.par_ref.at_ref, bf16[42,2,6,2,512]{4,3,2,1,0:T(2,128)(2,1)S(1)} %bitcast.20), custom_call_target="tpu_custom_call" | custom-call | flops 1000000000 | bytes 3000000 | tf_op jit(solution)/shard_map/pack/pallas_call | solution.py:59
  2.0 0.5 %collective-permute-start.2 = (bf16[432,512]{1,0:T(8,128)(2,1)S(1)}, bf16[432,512]{1,0:T(8,128)(2,1)S(1)}, u32[]{:S(2)}, u32[]{:S(2)}) collective-permute-start(bf16[432,512]{1,0:T(8,128)(2,1)S(1)} %get-tuple-element.28.own), channel_id=1, source_target_pairs={{0,4},{4,0},{8,12},{12,8},{16,20},{20,16},{24,28},{28,24},{1,5},{5... | collective-permute-start | bytes 1327112 | tf_op jit(solution)/shard_map/ppermute | solution.py:413
  2.5 3.6 %collective-permute-start.3 = (bf16[432,512]{1,0:T(8,128)(2,1)S(1)}, bf16[432,512]{1,0:T(8,128)(2,1)S(1)}, u32[]{:S(2)}, u32[]{:S(2)}) collective-permute-start(bf16[432,512]{1,0:T(8,128)(2,1)S(1)} %get-tuple-element.31.far), channel_id=1, source_target_pairs={{0,28},{4,8},{8,4},{12,16},{16,12},{20,24},{24,20},{28,0},{1,29},{... | collective-permute-start | bytes 1327112 | tf_op jit(solution)/shard_map/ppermute | solution.py:412
  6.1 1.6 %collective-permute-start = (bf16[2,36,512]{2,1,0:T(8,128)(2,1)S(1)}, bf16[2,36,512]{2,1,0:T(8,128)(2,1)S(1)}, u32[]{:S(2)}, u32[]{:S(2)}) collective-permute-start(bf16[2,36,512]{2,1,0:T(8,128)(2,1)S(1)} %get-tuple-element.22.bot_ref), channel_id=1, source_target_pairs={{0,1},{1,2},{2,3},{3,0},{4,5},{5,6},{6,7},{7,4},{8,9},{9,10},{10,1... | collective-permute-start | bytes 221192 | tf_op jit(solution)/shard_map/ppermute | solution.py:414
  7.6 2.2 %collective-permute-start.1 = (bf16[2,36,512]{2,1,0:T(8,128)(2,1)S(1)}, bf16[2,36,512]{2,1,0:T(8,128)(2,1)S(1)}, u32[]{:S(2)}, u32[]{:S(2)}) collective-permute-start(bf16[2,36,512]{2,1,0:T(8,128)(2,1)S(1)} %get-tuple-element.23.top_ref), channel_id=1, source_target_pairs={{0,3},{1,0},{2,1},{3,2},{4,7},{5,4},{6,5},{7,6},{8,11},{9,8},{10,9... | collective-permute-start | bytes 221192 | tf_op jit(solution)/shard_map/ppermute | solution.py:415
  9.9 0.0 copy-done.7
  9.9 0.0 copy-done.8
  9.9 0.0 copy-start
  9.9 0.0 copy-start.1
  9.9 0.0 copy-start.2
  9.9 0.0 copy-start.3
  9.9 0.0 copy-start.4
  9.9 0.0 copy-start.5
  9.9 3.3 %prep.1 = (f32[16,72,144]{2,1,0:T(8,128)S(1)}, f32[16,72,144]{2,1,0:T(8,128)S(1)}, f32[6,72,144]{2,1,0:T(8,128)S(1)}, f32[6,72,144]{2,1,0:T(8,128)S(1)}, f32[4,72,144]{2,1,0:T(8,128)S(1)}) custom-call(s32[3]{0:T(128)S(1)} %pad_add_fusion.par_ref.at_ref, s32[168,96]{1,0:T(8,128)S(1)} %copy-done.7, f32[16,759]{1,0:T(8,128)S(1)} %bitcast.21), custom_call_target="tpu_custom_call" | custom-call | flops 2000000000 | bytes 6000000 | tf_op jit(solution)/shard_map/prep/pallas_call | solution.py:181
  13.3 0.0 collective-permute-done.above_ref
  13.3 0.0 collective-permute-done.1.below_ref
  13.4 0.1 collective-permute-start.4
  13.5 0.8 %collective-permute-start.5 = (bf16[144,512]{1,0:T(8,128)(2,1)S(1)}, bf16[144,512]{1,0:T(8,128)(2,1)S(1)}, u32[]{:S(2)}, u32[]{:S(2)}) collective-permute-start(bf16[144,512]{1,0:T(8,128)(2,1)S(1)} %get-tuple-element.33.e_far), channel_id=1, source_target_pairs={{0,28},{4,8},{8,4},{12,16},{16,12},{20,24},{24,20},{28,0},{1,29},{... | collective-permute-start | bytes 442376 | tf_op jit(solution)/shard_map/ppermute | solution.py:420
  14.2 0.0 collective-permute-done.2.halo
  14.3 0.0 copy-done
  14.3 0.0 copy-done.1
  14.3 0.0 copy-done.2
  14.3 0.0 copy-done.3
  14.3 0.0 copy-done.4
  14.3 0.0 copy-done.5
  14.3 6.4 %near.1.near_res = bf16[36,6,2,512]{3,2,1,0:T(2,128)(2,1)S(1)} custom-call(bf16[432,512]{1,0:T(8,128)(2,1)S(1)} %get-tuple-element.28.own, bf16[432,512]{1,0:T(8,128)(2,1)S(1)} %collective-permute-done.2.halo, f32[16,72,144]{2,1,0:T(8,128)S(1)} %get-tuple-element.29.bias.refs_0_, f32[6,72,144]{2,1,0:T(8,128)S(1)} %get-tuple-element.30.mask, ...), custom_call_target="tpu_custom_call" | custom-call | flops 1000000000 | bytes 3000000 | tf_op jit(solution)/shard_map/near/pallas_call | solution.py:362
  20.7 0.0 collective-permute-done.4.e_near_halo
  20.7 0.0 collective-permute-done.5.e_far_halo
  20.7 0.0 collective-permute-done.3.far_halo
  20.7 10.2 %last.1 = bf16[42,2,6,2,512]{4,3,2,1,0:T(2,128)(2,1)} custom-call(s32[3]{0:T(128)S(1)} %pad_add_fusion.par_ref.at_ref, bf16[36,6,2,512]{3,2,1,0:T(2,128)(2,1)S(1)} %near.1.near_res, bf16[432,512]{1,0:T(8,128)(2,1)S(1)} %get-tuple-element.31.far, bf16[432,512]{1,0:T(8,128)(2,1)S(1)} %collective-permute-done.3.far_halo, ...), custom_call_target="tpu_custom_call" | custom-call | flops 12000000000 | bytes 36000000 | tf_op jit(solution)/shard_map/last/pallas_call | solution.py:378
  (1 shorter events, 0.0 us)
Async XLA Ops:
  0.1 1.2 %copy-start.6 = (bf16[1,2,42,12,512]{4,1,3,2,0:T(2,128)(2,1)S(1)}, bf16[1,2,42,12,512]{4,1,3,2,0:T(2,128)(2,1)}, u32[]{:S(2)}) copy-start(bf16[1,2,42,12,512]{4,1,3,2,0:T(2,128)(2,1)} %param.9) | copy-start | bytes 3096580
  1.3 8.6 %copy-start.7 = (s32[168,96]{1,0:T(8,128)S(1)}, s32[168,96]{1,0:T(8,128)}, u32[]{:S(2)}) copy-start(s32[168,96]{1,0:T(8,128)} %gid_ref.1) | copy-start | bytes 193540
  1.3 8.6 %copy-start.8 = (f32[759,16]{0,1:T(8,128)S(1)}, f32[759,16]{0,1:T(8,128)}, u32[]{:S(2)}) copy-start(f32[759,16]{0,1:T(8,128)} %param.11) | copy-start | bytes 145732
  2.0 12.3 %collective-permute-start.2 = (bf16[432,512]{1,0:T(8,128)(2,1)S(1)}, bf16[432,512]{1,0:T(8,128)(2,1)S(1)}, u32[]{:S(2)}, u32[]{:S(2)}) collective-permute-start(bf16[432,512]{1,0:T(8,128)(2,1)S(1)} %get-tuple-element.28.own), channel_id=1, source_target_pairs={{0,4},{4,0},{8,12},{12,8},{16,20},{20,16},{24,28},{28,24},{1,5},{5... | collective-permute-start | bytes 1327112 | tf_op jit(solution)/shard_map/ppermute | solution.py:413
  2.5 18.2 %collective-permute-start.3 = (bf16[432,512]{1,0:T(8,128)(2,1)S(1)}, bf16[432,512]{1,0:T(8,128)(2,1)S(1)}, u32[]{:S(2)}, u32[]{:S(2)}) collective-permute-start(bf16[432,512]{1,0:T(8,128)(2,1)S(1)} %get-tuple-element.31.far), channel_id=1, source_target_pairs={{0,28},{4,8},{8,4},{12,16},{16,12},{20,24},{24,20},{28,0},{1,29},{... | collective-permute-start | bytes 1327112 | tf_op jit(solution)/shard_map/ppermute | solution.py:412
  6.1 7.2 %collective-permute-start = (bf16[2,36,512]{2,1,0:T(8,128)(2,1)S(1)}, bf16[2,36,512]{2,1,0:T(8,128)(2,1)S(1)}, u32[]{:S(2)}, u32[]{:S(2)}) collective-permute-start(bf16[2,36,512]{2,1,0:T(8,128)(2,1)S(1)} %get-tuple-element.22.bot_ref), channel_id=1, source_target_pairs={{0,1},{1,2},{2,3},{3,0},{4,5},{5,6},{6,7},{7,4},{8,9},{9,10},{10,1... | collective-permute-start | bytes 221192 | tf_op jit(solution)/shard_map/ppermute | solution.py:414
  7.6 5.7 %collective-permute-start.1 = (bf16[2,36,512]{2,1,0:T(8,128)(2,1)S(1)}, bf16[2,36,512]{2,1,0:T(8,128)(2,1)S(1)}, u32[]{:S(2)}, u32[]{:S(2)}) collective-permute-start(bf16[2,36,512]{2,1,0:T(8,128)(2,1)S(1)} %get-tuple-element.23.top_ref), channel_id=1, source_target_pairs={{0,3},{1,0},{2,1},{3,2},{4,7},{5,4},{6,5},{7,6},{8,11},{9,8},{10,9... | collective-permute-start | bytes 221192 | tf_op jit(solution)/shard_map/ppermute | solution.py:415
  9.9 4.4 %copy-start = (bf16[512,2048]{1,0:T(8,128)(2,1)S(1)}, bf16[512,2048]{1,0:T(8,128)(2,1)}, u32[]{:S(2)}) copy-start(bf16[512,2048]{1,0:T(8,128)(2,1)} %refs_6_.1) | copy-start | bytes 6291460
  9.9 4.4 %copy-start.1 = (bf16[2048,512]{1,0:T(8,128)(2,1)S(1)}, bf16[2048,512]{1,0:T(8,128)(2,1)}, u32[]{:S(2)}) copy-start(bf16[2048,512]{1,0:T(8,128)(2,1)} %refs_7_.1) | copy-start | bytes 6291460
  9.9 4.4 %copy-start.2 = (bf16[512,1536]{1,0:T(8,128)(2,1)S(1)}, bf16[512,1536]{1,0:T(8,128)(2,1)}, u32[]{:S(2)}) copy-start(bf16[512,1536]{1,0:T(8,128)(2,1)} %refs_4_.1) | copy-start | bytes 4718596
  9.9 4.4 %copy-start.3 = (bf16[512,512]{1,0:T(8,128)(2,1)S(1)}, bf16[512,512]{1,0:T(8,128)(2,1)}, u32[]{:S(2)}) copy-start(bf16[512,512]{1,0:T(8,128)(2,1)} %refs_5_.1) | copy-start | bytes 1572868
  9.9 4.4 %copy-start.4 = (f32[512]{0:T(512)S(1)}, f32[512]{0:T(512)}, u32[]{:S(2)}) copy-start(f32[512]{0:T(512)} %param.14) | copy-start | bytes 6148
  9.9 4.4 %copy-start.5 = (f32[512]{0:T(512)S(1)}, f32[512]{0:T(512)}, u32[]{:S(2)}) copy-start(f32[512]{0:T(512)} %param.17) | copy-start | bytes 6148
  13.4 7.3 %collective-permute-start.4 = (bf16[144,512]{1,0:T(8,128)(2,1)S(1)}, bf16[144,512]{1,0:T(8,128)(2,1)S(1)}, u32[]{:S(2)}, u32[]{:S(2)}) collective-permute-start(bf16[144,512]{1,0:T(8,128)(2,1)S(1)} %get-tuple-element.32.e_near), channel_id=1, source_target_pairs={{0,4},{4,0},{8,12},{12,8},{16,20},{20,16},{24,28},{28,24},{1,5},{5... | collective-permute-start | bytes 442376 | tf_op jit(solution)/shard_map/ppermute | solution.py:419
  13.5 7.2 %collective-permute-start.5 = (bf16[144,512]{1,0:T(8,128)(2,1)S(1)}, bf16[144,512]{1,0:T(8,128)(2,1)S(1)}, u32[]{:S(2)}, u32[]{:S(2)}) collective-permute-start(bf16[144,512]{1,0:T(8,128)(2,1)S(1)} %get-tuple-element.33.e_far), channel_id=1, source_target_pairs={{0,28},{4,8},{8,4},{12,16},{16,12},{20,24},{24,20},{28,0},{1,29},{... | collective-permute-start | bytes 442376 | tf_op jit(solution)/shard_map/ppermute | solution.py:420

commit v5 on v4

--- a/solution.py
+++ b/solution.py
@@ -93,7 +93,22 @@
 
 
 def prep_kernel(
-    at_ref, gid_ref, table_ref, bias_near, bias_far, mask_near, mask_far, mask_edge, wide, kinds
+    at_ref,
+    gid_ref,
+    table_ref,
+    near_own,
+    near_halo,
+    w_qkv,
+    bias_near,
+    bias_far,
+    mask_near,
+    mask_far,
+    mask_edge,
+    q,
+    k,
+    v,
+    wide,
+    kinds,
 ):
     heads, offsets = table_ref.shape
     nw, nh = 2 * WIN_LON - 1, 2 * WIN_LAT - 1
@@ -131,6 +146,8 @@
                 both = pltpu.roll(both, SPREAD - start, 1)
             both = both.reshape(heads, 16, SPREAD)
             out[:, h * ROW : (h + 1) * ROW, :] = both[:, :ROW, :KEYS]
+    scale = LOG2E / (w_qkv.shape[0] // heads) ** 0.5
+    project([(near_own, near_halo, None, None, 0, 0, near_own.shape[0])], w_qkv, q, k, v, scale)
     total, around = gid_ref.shape
     wins = mask_near.shape[0] + 2
     lat_rows = (wins - 1) * WIN_LAT
@@ -175,16 +192,18 @@
                 mask_far[k - 1] = mask
 
 
-def prep(at, group_ids, table, wins):
+def prep(at, group_ids, table, own, halo, w_qkv, wins):
+    rows, d = own.shape
     heads, offsets = table.shape
     count = -(-offsets // 256) * 256
     return pl.pallas_call(
         prep_kernel,
-        in_specs=[pl.BlockSpec(memory_space=pltpu.SMEM)] + vmem(2),
-        out_specs=vmem(5),
+        in_specs=[pl.BlockSpec(memory_space=pltpu.SMEM)] + vmem(5),
+        out_specs=vmem(8),
         out_shape=[jax.ShapeDtypeStruct((heads, HALF, KEYS), F32)] * 2
         + [jax.ShapeDtypeStruct((wins - 2, HALF, KEYS), F32)] * 2
-        + [jax.ShapeDtypeStruct((4, HALF, KEYS), F32)],
+        + [jax.ShapeDtypeStruct((4, HALF, KEYS), F32), jax.ShapeDtypeStruct((rows, d), F32)]
+        + [jax.ShapeDtypeStruct((rows // HALF, KEYS, d), BF16)] * 2,
         scratch_shapes=[
             pltpu.VMEM((heads, count), F32),
             pltpu.VMEM((3, heads * 16, SPREAD), F32),
@@ -192,7 +211,7 @@
         compiler_params=params(),
         cost_estimate=cost(PREP_US),
         name="prep",
-    )(at, group_ids, table)
+    )(at, group_ids, table, own, halo, w_qkv)
 
 
 def norm_rows(value, gain):
@@ -223,16 +242,9 @@
     return num / den
 
 
-def layer_body(blocks, weights, scratch):
-    w_qkv, w_proj, w_in, w_out, gain_attn, gain_mlp = weights
-    q_scr, k_scr, v_scr, o_scr, mid_scr, acc_scr = scratch
-    d = w_proj.shape[0]
-    heads = blocks[0][2].shape[0]
-    hd = d // heads
-    lanes = GROUP * hd
-    groups = heads // GROUP
-    scale = LOG2E / hd**0.5
-    step = 2 * lanes
+def project(blocks, w_qkv, q_scr, k_scr, v_scr, scale):
+    d = w_qkv.shape[0]
+    step = 256
     asking = jnp.concatenate([own[q_lo : q_lo + n, :] for own, _, _, _, _, q_lo, n in blocks], 0)
     rows = jnp.concatenate([ref[...] for own, halo, *_ in blocks for ref in (own, halo)], 0)
     for c in range(0, d, step):
@@ -250,6 +262,19 @@
                     scr[wi, :, c : c + step] = jnp.concatenate([a, b], 0).astype(BF16)
                     wi += 1
                 at += 2 * size
+
+
+def layer_body(blocks, weights, scratch):
+    w_qkv, w_proj, w_in, w_out, gain_attn, gain_mlp = weights
+    q_scr, k_scr, v_scr, o_scr, mid_scr, acc_scr = scratch
+    d = w_proj.shape[0]
+    heads = blocks[0][2].shape[0]
+    hd = d // heads
+    lanes = GROUP * hd
+    groups = heads // GROUP
+    scale = LOG2E / hd**0.5
+    if w_qkv is not None:
+        project(blocks, w_qkv, q_scr, k_scr, v_scr, scale)
     base = 0
     wi = 0
     for own, halo, bias, mask_ref, mask_at, q_lo, q_rows in blocks:
@@ -293,10 +318,10 @@
     return mid_scr[...].astype(F32) + norm_rows(acc_scr[...], gain_mlp[...])
 
 
-def near_kernel(own, halo, bias, mask, *refs):
-    weights, out, scratch = refs[:6], refs[6], refs[7:]
+def near_kernel(own, q, k, v, bias, mask, *refs):
+    weights, out, scratch = (None, *refs[:5]), refs[5], (q, k, v, *refs[6:])
     rows, d = own.shape
-    res = layer_body([(own, halo, bias, mask, 0, 0, rows)], weights, scratch)
+    res = layer_body([(own, own, bias, mask, 0, 0, rows)], weights, scratch)
     out[...] = res.astype(BF16).reshape(out.shape)
 
 
@@ -356,19 +381,19 @@
     ]
 
 
-def near_layer(own, halo, bias, mask, weights):
+def near_layer(own, qkv, bias, mask, weights):
     rows, d = own.shape
     shape = (rows // ROW, SHIFT_LON, WIN_LEV, d)
     return pl.pallas_call(
         near_kernel,
-        in_specs=vmem(10),
+        in_specs=vmem(11),
         out_specs=vmem(1)[0],
         out_shape=jax.ShapeDtypeStruct(shape, BF16),
-        scratch_shapes=layer_scratch(rows, rows // HALF, weights),
+        scratch_shapes=layer_scratch(rows, rows // HALF, weights)[3:],
         compiler_params=params(),
         cost_estimate=cost(NEAR_US),
         name="near",
-    )(own, halo, bias, mask, *weights)
+    )(own, *qkv, bias, mask, *weights[1:])
 
 
 def last_layer(par, near_res, far, far_halo, edges, bias, masks, weights):
@@ -413,14 +438,16 @@
     near_halo = lax.ppermute(near, "lon", near_pairs)
     above = lax.ppermute(bot, "lat", down_pairs)
     below = lax.ppermute(top, "lat", up_pairs)
-    bias_near, bias_far, mask_near, mask_far, mask_edge = prep(at, group_ids, bias_table.T, wins)
+    bias_near, bias_far, mask_near, mask_far, mask_edge, *qkv = prep(
+        at, group_ids, bias_table.T, near, near_halo, w_qkv, wins
+    )
     above, below, bias_near = lax.optimization_barrier((above, below, bias_near))
     edge_near, edge_far = edge_pack(above, top, bot, below)
     edge_near_halo = lax.ppermute(edge_near, "lon", near_pairs)
     edge_far_halo = lax.ppermute(edge_far, "lon", far_pairs)
     weights = [w_qkv, w_proj, w_in, w_out, gain_attn.reshape(1, -1), gain_mlp.reshape(1, -1)]
     near, edge_near = lax.optimization_barrier((near, edge_near))
-    near_res = near_layer(near, near_halo, bias_near, mask_near, weights)
+    near_res = near_layer(near, qkv, bias_near, mask_near, weights)
     out = last_layer(
         at,
         near_res,

time: 31.2 us -> 31.5 us (level)
  waiting for transfers between devices: 0.02 us -> 0.73 us
    pallas_call x1, Pallas kernels: 6.36 us -> 5.37 us  [near_layer(): pl.pallas_call(near_kernel, in_specs=vmem(11), out_specs=vmem(1)[0], out_...]
    ppermute x1, waiting for transfers between devices: 0.01 us -> 0.71 us  [per_device(): edge_far_halo = lax.ppermute(edge_far, 'lon', far_pairs)]
    pallas_call x1, Pallas kernels: 3.35 us -> 4 us  [prep(): pl.pallas_call(prep_kernel, in_specs=[pl.BlockSpec(memory_space=pltpu.SME...]
  transfers between devices with their start and end apart: 6 -> 6, of which waited for: 0 -> 1; matrix products, arithmetic and copies ran while one was open for 0% -> 0% of each run, Pallas kernels for 31% -> 30%
where the time goes in v5:
time: 31.5 us; the launch traced here: 31.3 us
  Pallas kernels  20.3 us (64%)
  starting transfers between devices  8.61 us (27%)
  local copies, waits for them, and re-layouts  1.26 us (4%)
  waiting for transfers between devices  0.73 us (2%)
    pallas_call x1, Pallas kernels, last_layer(): pl.pallas_call(last_kernel, in_specs=[pl.BlockSpec(memory_space=pltpu.SME...  10.2 us
    pallas_call x1, Pallas kernels, near_layer(): pl.pallas_call(near_kernel, in_specs=vmem(11), out_specs=vmem(1)[0], out_...  5.37 us
    pallas_call x1, Pallas kernels, prep(): pl.pallas_call(prep_kernel, in_specs=[pl.BlockSpec(memory_space=pltpu.SME...  4 us
    ppermute x1, starting transfers between devices, per_device(): far_halo = lax.ppermute(far, 'lon', far_pairs)  3.56 us
    ppermute x1, starting transfers between devices, per_device(): below = lax.ppermute(top, 'lat', up_pairs)  2.25 us
    ppermute x1, starting transfers between devices, per_device(): above = lax.ppermute(bot, 'lat', down_pairs)  1.58 us
    unnamed x18, local copies, waits for them, and re-layouts  1.26 us
    ppermute x1, waiting for transfers between devices, per_device(): edge_far_halo = lax.ppermute(edge_far, 'lon', far_pairs)  0.71 us
  transfers between devices with their start and end apart: 6, of which 1 were waited for; matrix products, arithmetic and copies ran while one was open for 0% of the time, Pallas kernels for 30%

profile of v5, /device:TPU:0, one launch (start us, length us, event | category | flops | bytes accessed | tf_op | source)
XLA Modules:
  0.0 31.3 jit_solution(10261974179901234927)
XLA Ops:
  0.0 0.1 pad_add_fusion.par_ref.at_ref
  0.1 0.0 copy-start.6
  0.1 1.2 %copy-done.6 = bf16[1,2,42,12,512]{4,1,3,2,0:T(2,128)(2,1)S(1)} copy-done((bf16[1,2,42,12,512]{4,1,3,2,0:T(2,128)(2,1)S(1)}, bf16[1,2,42,12,512]{4,1,3,2,0:T(2,128)(2,1)}, u32[]{:S(2)}) %copy-start.6) | copy-done | bytes 1032216
  1.3 0.0 copy-start.5
  1.3 0.0 copy-start.7
  1.3 0.0 copy-start.8
  1.3 0.7 %pack.1 = (bf16[432,512]{1,0:T(8,128)(2,1)S(1)}, bf16[432,512]{1,0:T(8,128)(2,1)S(1)}, bf16[2,36,512]{2,1,0:T(8,128)(2,1)S(1)}, bf16[2,36,512]{2,1,0:T(8,128)(2,1)S(1)}) custom-call(s32[3]{0:T(128)S(1)} %pad_add_fusion.par_ref.at_ref, bf16[42,2,6,2,512]{4,3,2,1,0:T(2,128)(2,1)S(1)} %bitcast.20), custom_call_target="tpu_custom_call" | custom-call | flops 1000000000 | bytes 3000000 | tf_op jit(solution)/shard_map/pack/pallas_call | solution.py:59
  2.0 0.5 %collective-permute-start.2 = (bf16[432,512]{1,0:T(8,128)(2,1)S(1)}, bf16[432,512]{1,0:T(8,128)(2,1)S(1)}, u32[]{:S(2)}, u32[]{:S(2)}) collective-permute-start(bf16[432,512]{1,0:T(8,128)(2,1)S(1)} %get-tuple-element.31.near_own.own), channel_id=1, source_target_pairs={{0,4},{4,0},{8,12},{12,8},{16,20},{20,16},{24,28},{28,24},{1,5},{5... | collective-permute-start | bytes 1327112 | tf_op jit(solution)/shard_map/ppermute | solution.py:438
  2.5 3.6 %collective-permute-start.3 = (bf16[432,512]{1,0:T(8,128)(2,1)S(1)}, bf16[432,512]{1,0:T(8,128)(2,1)S(1)}, u32[]{:S(2)}, u32[]{:S(2)}) collective-permute-start(bf16[432,512]{1,0:T(8,128)(2,1)S(1)} %get-tuple-element.37.far), channel_id=1, source_target_pairs={{0,28},{4,8},{8,4},{12,16},{16,12},{20,24},{24,20},{28,0},{1,29},{... | collective-permute-start | bytes 1327112 | tf_op jit(solution)/shard_map/ppermute | solution.py:437
  6.1 1.6 %collective-permute-start = (bf16[2,36,512]{2,1,0:T(8,128)(2,1)S(1)}, bf16[2,36,512]{2,1,0:T(8,128)(2,1)S(1)}, u32[]{:S(2)}, u32[]{:S(2)}) collective-permute-start(bf16[2,36,512]{2,1,0:T(8,128)(2,1)S(1)} %get-tuple-element.25.bot_ref), channel_id=1, source_target_pairs={{0,1},{1,2},{2,3},{3,0},{4,5},{5,6},{6,7},{7,4},{8,9},{9,10},{10,1... | collective-permute-start | bytes 221192 | tf_op jit(solution)/shard_map/ppermute | solution.py:439
  7.6 2.2 %collective-permute-start.1 = (bf16[2,36,512]{2,1,0:T(8,128)(2,1)S(1)}, bf16[2,36,512]{2,1,0:T(8,128)(2,1)S(1)}, u32[]{:S(2)}, u32[]{:S(2)}) collective-permute-start(bf16[2,36,512]{2,1,0:T(8,128)(2,1)S(1)} %get-tuple-element.26.top_ref), channel_id=1, source_target_pairs={{0,3},{1,0},{2,1},{3,2},{4,7},{5,4},{6,5},{7,6},{8,11},{9,8},{10,9... | collective-permute-start | bytes 221192 | tf_op jit(solution)/shard_map/ppermute | solution.py:440
  9.9 0.0 collective-permute-done.2.near_halo
  9.9 0.0 copy-done.5
  9.9 0.0 copy-done.7
  9.9 0.0 copy-done.8
  9.9 0.0 copy-start
  9.9 0.0 copy-start.1
  9.9 0.0 copy-start.2
  9.9 0.0 copy-start.3
  10.0 0.0 copy-start.4
  10.0 4.0 %prep.1 = (f32[16,72,144]{2,1,0:T(8,128)S(1)}, f32[16,72,144]{2,1,0:T(8,128)S(1)}, f32[6,72,144]{2,1,0:T(8,128)S(1)}, f32[6,72,144]{2,1,0:T(8,128)S(1)}, f32[4,7...) custom-call(s32[3]{0:T(128)S(1)} %pad_add_fusion.par_ref.at_ref, ...), custom_call_target="tpu_custom_call" | custom-call | flops 2000000000 | bytes 6000000 | tf_op jit(solution)/shard_map/prep/pallas_call | solution.py:199
  14.0 0.0 collective-permute-done.above_ref
  14.0 0.0 collective-permute-done.1.below_ref
  14.0 0.1 edge_pack.1
  14.0 0.1 collective-permute-start.4
  14.1 0.6 %collective-permute-start.5 = (bf16[144,512]{1,0:T(8,128)(2,1)S(1)}, bf16[144,512]{1,0:T(8,128)(2,1)S(1)}, u32[]{:S(2)}, u32[]{:S(2)}) collective-permute-start(bf16[144,512]{1,0:T(8,128)(2,1)S(1)} %get-tuple-element.39.e_far), channel_id=1, source_target_pairs={{0,28},{4,8},{8,4},{12,16},{16,12},{20,24},{24,20},{28,0},{1,29},{... | collective-permute-start | bytes 442376 | tf_op jit(solution)/shard_map/ppermute | solution.py:447
  14.8 0.0 copy-done
  14.8 0.0 copy-done.1
  14.8 0.0 copy-done.2
  14.8 0.0 copy-done.3
  14.8 0.0 copy-done.4
  14.8 5.4 %near.1.near_res = bf16[36,6,2,512]{3,2,1,0:T(2,128)(2,1)S(1)} custom-call(bf16[432,512]{1,0:T(8,128)(2,1)S(1)} %get-tuple-element.31.near_own.own, f32[432,512]{1,0:T(8,128)S(1)} %get-tuple-element.32.q, bf16[6,144,512]{2,1,0:T(8,128)(2,1)S(1)} %get-tuple-element.33.k, bf16[6,144,512]{2,1,0:T(8,128)(2,1)S(1)} %get-tuple-element.34.v, ...), custom_call_target="tpu_custom_call" | custom-call | flops 1000000000 | bytes 3000000 | tf_op jit(solution)/shard_map/near/pallas_call | solution.py:387
  20.2 0.0 collective-permute-done.3.far_halo
  20.2 0.0 collective-permute-done.4.e_near_halo
  20.2 0.7 %collective-permute-done.5.e_far_halo = bf16[144,512]{1,0:T(8,128)(2,1)S(1)} collective-permute-done((bf16[144,512]{1,0:T(8,128)(2,1)S(1)}, bf16[144,512]{1,0:T(8,128)(2,1)S(1)}, u32[]{:S(2)}, u32[]{:S(2)}) %collective-permute-start.5) | collective-permute-done | bytes 147488 | tf_op jit(solution)/shard_map/ppermute | solution.py:447
  20.9 10.2 %last.1 = bf16[42,2,6,2,512]{4,3,2,1,0:T(2,128)(2,1)} custom-call(s32[3]{0:T(128)S(1)} %pad_add_fusion.par_ref.at_ref, bf16[36,6,2,512]{3,2,1,0:T(2,128)(2,1)S(1)} %near.1.near_res, bf16[432,512]{1,0:T(8,128)(2,1)S(1)} %get-tuple-element.37.far, bf16[432,512]{1,0:T(8,128)(2,1)S(1)} %collective-permute-done.3.far_halo, ...), custom_call_target="tpu_custom_call" | custom-call | flops 12000000000 | bytes 36000000 | tf_op jit(solution)/shard_map/last/pallas_call | solution.py:403
Async XLA Ops:
  0.1 1.2 %copy-start.6 = (bf16[1,2,42,12,512]{4,1,3,2,0:T(2,128)(2,1)S(1)}, bf16[1,2,42,12,512]{4,1,3,2,0:T(2,128)(2,1)}, u32[]{:S(2)}) copy-start(bf16[1,2,42,12,512]{4,1,3,2,0:T(2,128)(2,1)} %param.9) | copy-start | bytes 3096580
  1.3 8.6 %copy-start.5 = (bf16[512,1536]{1,0:T(8,128)(2,1)S(1)}, bf16[512,1536]{1,0:T(8,128)(2,1)}, u32[]{:S(2)}) copy-start(bf16[512,1536]{1,0:T(8,128)(2,1)} %refs_4_.1) | copy-start | bytes 4718596
  1.3 8.6 %copy-start.7 = (s32[168,96]{1,0:T(8,128)S(1)}, s32[168,96]{1,0:T(8,128)}, u32[]{:S(2)}) copy-start(s32[168,96]{1,0:T(8,128)} %gid_ref.1) | copy-start | bytes 193540
  1.3 8.6 %copy-start.8 = (f32[759,16]{0,1:T(8,128)S(1)}, f32[759,16]{0,1:T(8,128)}, u32[]{:S(2)}) copy-start(f32[759,16]{0,1:T(8,128)} %param.11) | copy-start | bytes 145732
  2.0 7.9 %collective-permute-start.2 = (bf16[432,512]{1,0:T(8,128)(2,1)S(1)}, bf16[432,512]{1,0:T(8,128)(2,1)S(1)}, u32[]{:S(2)}, u32[]{:S(2)}) collective-permute-start(bf16[432,512]{1,0:T(8,128)(2,1)S(1)} %get-tuple-element.31.near_own.own), channel_id=1, source_target_pairs={{0,4},{4,0},{8,12},{12,8},{16,20},{20,16},{24,28},{28,24},{1,5},{5... | collective-permute-start | bytes 1327112 | tf_op jit(solution)/shard_map/ppermute | solution.py:438
  2.5 17.7 %collective-permute-start.3 = (bf16[432,512]{1,0:T(8,128)(2,1)S(1)}, bf16[432,512]{1,0:T(8,128)(2,1)S(1)}, u32[]{:S(2)}, u32[]{:S(2)}) collective-permute-start(bf16[432,512]{1,0:T(8,128)(2,1)S(1)} %get-tuple-element.37.far), channel_id=1, source_target_pairs={{0,28},{4,8},{8,4},{12,16},{16,12},{20,24},{24,20},{28,0},{1,29},{... | collective-permute-start | bytes 1327112 | tf_op jit(solution)/shard_map/ppermute | solution.py:437
  6.1 7.9 %collective-permute-start = (bf16[2,36,512]{2,1,0:T(8,128)(2,1)S(1)}, bf16[2,36,512]{2,1,0:T(8,128)(2,1)S(1)}, u32[]{:S(2)}, u32[]{:S(2)}) collective-permute-start(bf16[2,36,512]{2,1,0:T(8,128)(2,1)S(1)} %get-tuple-element.25.bot_ref), channel_id=1, source_target_pairs={{0,1},{1,2},{2,3},{3,0},{4,5},{5,6},{6,7},{7,4},{8,9},{9,10},{10,1... | collective-permute-start | bytes 221192 | tf_op jit(solution)/shard_map/ppermute | solution.py:439
  7.6 6.3 %collective-permute-start.1 = (bf16[2,36,512]{2,1,0:T(8,128)(2,1)S(1)}, bf16[2,36,512]{2,1,0:T(8,128)(2,1)S(1)}, u32[]{:S(2)}, u32[]{:S(2)}) collective-permute-start(bf16[2,36,512]{2,1,0:T(8,128)(2,1)S(1)} %get-tuple-element.26.top_ref), channel_id=1, source_target_pairs={{0,3},{1,0},{2,1},{3,2},{4,7},{5,4},{6,5},{7,6},{8,11},{9,8},{10,9... | collective-permute-start | bytes 221192 | tf_op jit(solution)/shard_map/ppermute | solution.py:440
  9.9 4.9 %copy-start = (bf16[512,2048]{1,0:T(8,128)(2,1)S(1)}, bf16[512,2048]{1,0:T(8,128)(2,1)}, u32[]{:S(2)}) copy-start(bf16[512,2048]{1,0:T(8,128)(2,1)} %refs_6_.1) | copy-start | bytes 6291460
  9.9 4.8 %copy-start.1 = (bf16[2048,512]{1,0:T(8,128)(2,1)S(1)}, bf16[2048,512]{1,0:T(8,128)(2,1)}, u32[]{:S(2)}) copy-start(bf16[2048,512]{1,0:T(8,128)(2,1)} %refs_7_.1) | copy-start | bytes 6291460
  9.9 4.8 %copy-start.2 = (bf16[512,512]{1,0:T(8,128)(2,1)S(1)}, bf16[512,512]{1,0:T(8,128)(2,1)}, u32[]{:S(2)}) copy-start(bf16[512,512]{1,0:T(8,128)(2,1)} %refs_5_.1) | copy-start | bytes 1572868
  9.9 4.8 %copy-start.3 = (f32[512]{0:T(512)S(1)}, f32[512]{0:T(512)}, u32[]{:S(2)}) copy-start(f32[512]{0:T(512)} %param.14) | copy-start | bytes 6148
  10.0 4.8 %copy-start.4 = (f32[512]{0:T(512)S(1)}, f32[512]{0:T(512)}, u32[]{:S(2)}) copy-start(f32[512]{0:T(512)} %param.17) | copy-start | bytes 6148
  14.0 6.1 %collective-permute-start.4 = (bf16[144,512]{1,0:T(8,128)(2,1)S(1)}, bf16[144,512]{1,0:T(8,128)(2,1)S(1)}, u32[]{:S(2)}, u32[]{:S(2)}) collective-permute-start(bf16[144,512]{1,0:T(8,128)(2,1)S(1)} %get-tuple-element.38.e_near), channel_id=1, source_target_pairs={{0,4},{4,0},{8,12},{12,8},{16,20},{20,16},{24,28},{28,24},{1,5},{5... | collective-permute-start | bytes 442376 | tf_op jit(solution)/shard_map/ppermute | solution.py:446
  14.1 6.8 %collective-permute-start.5 = (bf16[144,512]{1,0:T(8,128)(2,1)S(1)}, bf16[144,512]{1,0:T(8,128)(2,1)S(1)}, u32[]{:S(2)}, u32[]{:S(2)}) collective-permute-start(bf16[144,512]{1,0:T(8,128)(2,1)S(1)} %get-tuple-element.39.e_far), channel_id=1, source_target_pairs={{0,28},{4,8},{8,4},{12,16},{16,12},{20,24},{24,20},{28,0},{1,29},{... | collective-permute-start | bytes 442376 | tf_op jit(solution)/shard_map/ppermute | solution.py:447
